TPU v7x, 512 devices: a whole 4x4x16 slice. The times are simulated.
512 devices in a mesh: row: 16 (over y, x), col: 32 (over z, core).
Axes of the slice: x: 4, y: 4, z: 16, core: 2. Of those that a mesh axis runs over, the one named last changes fastest.
Arguments:
- points: bfloat16 [262144, 256], P(('col', 'row')), may hold values from -6 to 6
- weights: bfloat16 [262144, 128], P(('col', 'row')), may hold values from -6 to 6
- near_blocks: int32 [2048, 16], P(('col', 'row')), may hold values from 0 to 2047, as said below
- proxies: bfloat16 [64, 256], replicated, may hold values from -6 to 6
Outputs:
- near_product: bfloat16 [262144, 128], P(('col', 'row'))
- factors: float32 [32768, 192], P(('col', 'row'))
Inputs may be any that keep to these rules, and one draw needn't show every extreme that they name: near_blocks[j, 0] = j; every entry of row j lies in the column group of j, that is in the same run of 64 blocks; entries may repeat.
All inputs are finite; a program needn't handle non-finite values.
Results may differ from a plain program's by a relative error of at most 0.01.
Values may be sent and summed in bfloat16 or wider, within the bound.
No kernel may reach another device: no remote copies, remote signals or barrier semaphores. Data moves between devices by JAX's collectives and lax.ppermute only.
A program may use at most 64 MiB of HBM per device.

v0:
```python
import jax
import jax.numpy as jnp
from jax import lax
from jax.sharding import PartitionSpec as P

DIM = 256
BLK = 128
NV = 128


def partner(value, axis, stride):
    mask = 2**stride
    pairs = [(source, source ^ mask) for source in range(lax.axis_size(axis))]
    return lax.ppermute(value, axis, pairs)


def kern_tile(left, right):
    cross = jnp.dot(left, right.T, preferred_element_type=jnp.float32)
    lnorm = jnp.sum(left.astype(jnp.float32) ** 2, axis=-1)
    rnorm = jnp.sum(right.astype(jnp.float32) ** 2, axis=-1)
    return jnp.exp(-(lnorm[:, None] + rnorm[None, :] - 2.0 * cross) * (2.0 / DIM))


def level_merge(lower_own, lower_other):
    high = lax.Precision.HIGHEST
    gram = jnp.dot(lower_own, lower_own.T, precision=high) + jnp.dot(
        lower_other, lower_other.T, precision=high
    )
    merged = jnp.linalg.cholesky(gram)
    transfer = lax.linalg.triangular_solve(merged, lower_own, left_side=True, lower=True).T
    return (merged, transfer)


def on_device(points, weights, near_blocks, proxies):
    n_local = near_blocks.shape[0]
    group_count = n_local * lax.axis_size("row")
    base = lax.axis_index("col") * group_count
    gathered = lax.all_gather(points, "row", axis=0, tiled=True)
    tblocks = gathered.reshape(group_count, BLK, DIM)
    local_ids = near_blocks - base
    sources = points.reshape(n_local, BLK, DIM)
    wblocks = weights.reshape(n_local, BLK, NV)
    targets = tblocks[local_ids]
    cross = jnp.einsum("jtad,jbd->jtab", targets, sources, preferred_element_type=jnp.float32)
    tnorm = jnp.sum(targets.astype(jnp.float32) ** 2, axis=-1)
    snorm = jnp.sum(sources.astype(jnp.float32) ** 2, axis=-1)
    dist = tnorm[:, :, :, None] + snorm[:, None, None, :] - 2.0 * cross
    tile = jnp.exp(-dist * (2.0 / DIM)).astype(jnp.bfloat16)
    contrib = jnp.einsum("jtab,jbv->jtav", tile, wblocks, preferred_element_type=jnp.float32)
    partial_value = jnp.zeros((group_count, BLK, NV), jnp.float32)
    partial_value = partial_value.at[local_ids.reshape(-1)].add(contrib.reshape(-1, BLK, NV))
    near_sum = lax.psum_scatter(
        partial_value.reshape(group_count * BLK, NV), "row", scatter_dimension=0, tiled=True
    )
    near_product = near_sum.astype(jnp.bfloat16)
    far = kern_tile(points, proxies)
    lower0 = jnp.linalg.cholesky(jnp.dot(far.T, far, precision=lax.Precision.HIGHEST))
    current = lower0
    transfers = []
    for level in range(2):
        sibling = partner(current, "col", level)
        current, transfer = level_merge(current, sibling)
        transfers.append(transfer)
    factors = jnp.concatenate([transfers[0], transfers[1], current.T], axis=1)
    return (near_product, factors)


def solution(mesh):
    placed = (P(("col", "row"), None), P(("col", "row"), None), P(("col", "row"), None), P())
    return jax.shard_map(
        on_device,
        mesh=mesh,
        in_specs=placed,
        out_specs=(P(("col", "row"), None), P(("col", "row"), None)),
        check_vma=False,
    )
```

profile of v0, /device:TPU:2, one launch (start us, length us, event | category | flops | bytes accessed | tf_op | source)
XLA Modules:
  0.0 213.1 jit_solution(5560618731934013219)
XLA Ops:
  7.2 0.0 copy-start
  7.2 0.0 all-gather.2.cloned.1.call-start
  7.2 0.7 all-gather.2.cloned.1.call-update
  7.9 0.0 reduce-scatter.2.cloned.1.call-start
  8.0 0.7 compare_select_fusion
  8.7 0.1 reshape.67
  8.7 0.1 reshape.77
  8.8 1.1 multiply_reduce_fusion.1
  9.9 72.4 %all-gather.2.cloned.1.call-done = bf16[8192,256]{1,0:T(8,128)(2,1)} async-done(((bf16[512,256]{1,0:T(8,128)(2,1)}), bf16[8192,256]{1,0:T(8,128)(2,1)}) %all-gather.2.cloned.1.call-update) | async-done | bytes 4194320 | tf_op jit(solution)/shard_map/all_gather | solution.py:38
  82.4 5.0 %gather_fusion = bf16[64,128,256]{2,1,0:T(8,128)(2,1)} fusion(bf16[64,128,256]{2,1,0:T(8,128)(2,1)} %bitcast.66, s32[1024]{0:T(1024)S(1)} %pad_clamp_fusion), kind=kCustom, calls=%fused_computation | custom fusion | bytes 8388864 | tf_op jit(solution)/shard_map/gather | solution.py:43
  87.3 0.0 copy-start.1
  87.3 3.4 %multiply_reduce_fusion = f32[4,16,128]{2,1,0:T(8,128)S(1)} fusion(bf16[4,16,128,256]{3,2,1,0:T(8,128)(2,1)} %bitcast.64), kind=kLoop, calls=%fused_computation.2 | loop fusion | flops 6283264 | bytes 4227072 | tf_op jit(solution)/shard_map/reduce_sum | solution.py:45
  90.7 0.0 copy-done
  90.7 0.0 copy-done.1
  90.7 4.9 %fusion = f32[4,16,128,128]{3,2,1,0:T(8,128)} fusion(bf16[4,128,128,1]{2,1,3,0:T(8,128)(2,1)S(1)} %bitcast.62, bf16[4,16,128,256]{3,2,1,0:T(8,128)(2,1)} %bitcast.65, bf16[4,128,256,1]{2,1,3,0:T(8,128)(2,1)S(1)} %bitcast.68, f32[4,128]{1,0:T(4,128)S(1)} %bitcast.69, f32[4,16,128]{2,1,0:T(8,128)S(1)} %multiply_reduce_fusion), kind=kOutput, calls=%fused_computation.4 | convolution fusion | flops 811597824 | bytes 8816640 | tf_op jit(solution)/shard_map/jtab,jbv->jtav/dot_general | solution.py:49
  95.6 2.5 %broadcast_in_dim.4 = f32[64,128,128]{2,1,0:T(8,128)} broadcast(f32[]{:T(128)} %constant.43.clone.1), dimensions={} | broadcast | bytes 4194308 | tf_op jit(solution)/shard_map/broadcast_in_dim | solution.py:50
  98.1 13.5 %scatter_fusion = f32[64,128,128]{2,1,0:T(8,128)} fusion(f32[64,128,128]{2,1,0:T(8,128)} %broadcast_in_dim.4, s32[64]{0:T(128)S(1)} %fusion.15, f32[64,128,128]{2,1,0:T(8,128)} %bitcast.67), kind=kCustom, calls=%fused_computation.1 | custom fusion | flops 1048576 | bytes 12583168 | tf_op jit(solution)/shard_map/scatter-add | solution.py:51
  111.6 0.0 copy-start.2
  111.6 0.0 reduce-scatter.2.cloned.1.call-update
  111.6 0.7 copy-done.2
  112.4 0.1 multiply_reduce_fusion.2
  112.5 0.2 fusion.4
  112.7 0.6 fusion.19
  113.3 0.1 copy.6
  113.4 5.8 %cholesky.59 = f32[64,64]{1,0:T(8,128)S(1)} custom-call(f32[64,64]{1,0:T(8,128)S(1)} %fusion.9), custom_call_target="Cholesky" | custom-call | tf_op jit(solution)/shard_map/jit(cholesky)/cholesky | solution.py:57
  119.3 0.6 compare_reduce_fusion.2
  119.9 0.7 fusion.10
  120.6 1.9 collective-permute-start
  122.5 0.2 fusion.20
  122.7 1.0 collective-permute-done
  123.7 0.2 convolution_add_fusion.1
  123.9 0.1 copy.9
  124.0 5.8 %cholesky.70 = f32[64,64]{1,0:T(8,128)S(1)} custom-call(f32[64,64]{1,0:T(8,128)S(1)} %fusion.8), custom_call_target="Cholesky" | custom-call | tf_op jit(solution)/shard_map/jit(cholesky)/cholesky | solution.py:29
  129.9 0.6 compare_reduce_fusion.1
  130.5 0.7 select_bitcast_fusion.1
  131.2 3.5 %collective-permute-start.1 = (f32[64,64]{1,0:T(8,128)S(1)}, f32[64,64]{1,0:T(8,128)S(1)}, u32[]{:S(2)}, u32[]{:S(2)}) collective-permute-start(f32[64,64]{1,0:T(8,128)S(1)} %get-tuple-element.7), channel_id=1, source_target_pairs={{0,2},{1,3},{2,0},{3,1},{4,6},{5,7},{6,4},{7,5},{8,10},{9,11},{10,... | collective-permute-start | bytes 49160 | tf_op jit(solution)/shard_map/ppermute | solution.py:14
  134.7 4.9 %custom-call.6 = f32[1,64,64]{1,2,0:T(8,128)S(1)} custom-call(f32[1,64,64]{2,1,0:T(8,128)S(1)} %get-tuple-element.6), custom_call_target="InvertDiagBlocksLowerTriangular" | custom-call | tf_op jit(solution)/shard_map/triangular_solve/custom-call.0 | solution.py:30
  139.6 0.2 fusion.21
  139.8 0.2 convolution_bitcast_fusion.1
  140.0 0.0 collective-permute-done.1
  140.0 0.2 convolution_add_fusion
  140.2 0.1 copy.13
  140.3 5.8 %cholesky.81 = f32[64,64]{1,0:T(8,128)S(1)} custom-call(f32[64,64]{1,0:T(8,128)S(1)} %fusion.6), custom_call_target="Cholesky" | custom-call | tf_op jit(solution)/shard_map/jit(cholesky)/cholesky | solution.py:29
  146.2 0.6 compare_reduce_fusion
  146.9 0.7 select_bitcast_fusion
  147.5 4.9 %custom-call.7 = f32[1,64,64]{1,2,0:T(8,128)S(1)} custom-call(f32[1,64,64]{2,1,0:T(8,128)S(1)} %get-tuple-element.10), custom_call_target="InvertDiagBlocksLowerTriangular" | custom-call | tf_op jit(solution)/shard_map/triangular_solve/custom-call.0 | solution.py:30
  152.4 0.3 convolution_bitcast_fusion
  152.7 0.7 copy.15
  153.4 51.2 %reduce-scatter.2.cloned.1.call-done = f32[512,128]{1,0:T(8,128)} async-done(((f32[8192,128]{1,0:T(8,128)}), f32[512,128]{1,0:T(8,128)}) %reduce-scatter.2.cloned.1.call-update) | async-done | bytes 262160 | tf_op jit(solution)/shard_map/reduce_scatter | solution.py:52
  204.6 1.6 convert_element_type.20
  (9 shorter events, 0.1 us)
Async XLA Ops:
  7.2 83.6 %copy-start = (bf16[512,128]{1,0:T(8,128)(2,1)S(1)}, bf16[512,128]{1,0:T(8,128)(2,1)}, u32[]{:S(2)}) copy-start(bf16[512,128]{1,0:T(8,128)(2,1)} %param.8) | copy-start | bytes 393220
  7.2 75.2 %all-gather.2.cloned.1.call-start = ((), (), s32[]{:S(2)}) async-start(), calls=%async_computation.1 | async-start | bytes 4456448 | tf_op jit(solution)/shard_map/all_gather | solution.py:38
  7.9 196.7 %reduce-scatter.2.cloned.1.call-start = ((), (), s32[]{:S(2)}) async-start(), calls=%async_computation.2 | async-start | bytes 4456448 | tf_op jit(solution)/shard_map/reduce_scatter | solution.py:52
  87.3 3.4 %copy-start.1 = (bf16[512,256]{1,0:T(8,128)(2,1)S(1)}, bf16[512,256]{1,0:T(8,128)(2,1)}, u32[]{:S(2)}) copy-start(bf16[512,256]{1,0:T(8,128)(2,1)} %param.7) | copy-start | bytes 786436
  111.6 0.8 copy-start.2
  120.6 3.1 %collective-permute-start = (f32[64,64]{1,0:T(8,128)S(1)}, f32[64,64]{1,0:T(8,128)S(1)}, u32[]{:S(2)}, u32[]{:S(2)}) collective-permute-start(f32[64,64]{1,0:T(8,128)S(1)} %fusion.10), channel_id=1, source_target_pairs={{0,1},{1,0},{2,3},{3,2},{4,5},{5,4},{6,7},{7,6},{8,9},{9,8},{10,11... | collective-permute-start | bytes 49160 | tf_op jit(solution)/shard_map/ppermute | solution.py:14
  131.2 8.9 %collective-permute-start.1 = (f32[64,64]{1,0:T(8,128)S(1)}, f32[64,64]{1,0:T(8,128)S(1)}, u32[]{:S(2)}, u32[]{:S(2)}) collective-permute-start(f32[64,64]{1,0:T(8,128)S(1)} %get-tuple-element.7), channel_id=1, source_target_pairs={{0,2},{1,3},{2,0},{3,1},{4,6},{5,7},{6,4},{7,5},{8,10},{9,11},{10,... | collective-permute-start | bytes 49160 | tf_op jit(solution)/shard_map/ppermute | solution.py:14
Sparse Core Ops, SparseCore 0:
  11.0 71.2 all-gather.1
  111.8 92.8 reduce-scatter.1
where the time goes:
time: 214 us; the launch traced here: 213 us
  waiting for transfers between devices  125 us (58%)
  other arithmetic  51.7 us (24%)
  between operations  14.3 us (7%)
  local copies, waits for them, and re-layouts  9.3 us (4%)
  matrix products  6.97 us (3%)
  starting transfers between devices  5.5 us (3%)
    all_gather x1, waiting for transfers between devices, on_device(): gathered = lax.all_gather(points, 'row', axis=0, tiled=True)  72.4 us
    reduce_scatter x1, waiting for transfers between devices, on_device(): lax.psum_scatter(partial_value.reshape(group_count * BLK, NV), 'row', sca...  51.2 us
    scatter-add x1, other arithmetic, on_device(): partial_value.at[local_ids.reshape(-1)].add(contrib.reshape(-1, BLK, NV))  13.5 us
    another operation x6, other arithmetic, level_merge(): merged = jnp.linalg.cholesky(gram)  13 us
    another operation x4, other arithmetic, level_merge(): lax.linalg.triangular_solve(merged, lower_own, left_side=True, lower=True)  11.1 us
    another operation x3, other arithmetic, on_device(): jnp.linalg.cholesky(jnp.dot(far.T, far, precision=lax.Precision.HIGHEST))  6.52 us
    ppermute x2, starting transfers between devices, partner(): return lax.ppermute(value, axis, pairs)  5.42 us
    gather x1, local copies, waits for them, and re-layouts, on_device(): targets = tblocks[local_ids]  4.97 us
  transfers between devices with their start and end apart: 4, of which 3 were waited for; matrix products, arithmetic and copies ran while one was open for 17% of the time, Pallas kernels for 0%

commit v1 on v0

v1 whole, which is shorter than its diff:
```python
import functools

import jax
import jax.numpy as jnp
import numpy as np
from jax import lax
from jax.experimental import pallas as pl
from jax.experimental.pallas import tpu as pltpu
from jax.sharding import PartitionSpec as P

DIM = 256
RANK = 64
BLK = 128
NV = 128
UNIT = 512
NB = 4
SIDE = 4
EXTRA = 16
ROWS = UNIT + EXTRA
GROUP = 64
LOG2E = 1.4426950408889634
MASKS = (0, 1, 3, 2)
NT = (((1,), (1,)), ((), ()))
HIGH = lax.Precision.HIGHEST
VMEM = 24 * 1024 * 1024


def dot_nt(a, b, precision=None):
    return lax.dot_general(a, b, NT, precision=precision, preferred_element_type=jnp.float32)


def split2(x):
    hi = x.astype(jnp.bfloat16)
    return hi, (x - hi.astype(jnp.float32)).astype(jnp.bfloat16)


def prepare_kernel(points, weights, near, proxies, send, gram, scale):
    p = points[...]
    send[:UNIT, :DIM] = p
    send[:UNIT, DIM:] = weights[...]
    f = p.astype(jnp.float32)
    hi, lo = split2(f * f)
    ones = jnp.ones((8, DIM), jnp.bfloat16)
    norm = dot_nt(ones, hi) + dot_nt(ones, lo)
    tall = jnp.ones((DIM, NV), jnp.bfloat16)
    column = jnp.dot(hi, tall, preferred_element_type=jnp.float32) + jnp.dot(
        lo, tall, preferred_element_type=jnp.float32
    )
    scale[...] = jnp.exp(column * (-2.0 / DIM))
    ids = near[...] & (GROUP - 1)
    lanes = lax.broadcasted_iota(jnp.int32, (NB, BLK), 1)
    counts = jnp.zeros((NB, BLK), jnp.float32)
    for t in range(near.shape[1]):
        counts = counts + jnp.where(ids[:, t : t + 1] == lanes, 1.0, 0.0)
    rows = jnp.concatenate([norm[0:1, b * BLK : (b + 1) * BLK] for b in range(NB)], axis=0)
    first = rows.astype(jnp.bfloat16).astype(jnp.float32)
    second = (rows - first).astype(jnp.bfloat16).astype(jnp.float32)
    third = rows - first - second
    extra = jnp.concatenate([counts, first, second, third], axis=0)
    send[UNIT:, :BLK] = extra.astype(jnp.bfloat16)
    send[UNIT:, BLK:] = jnp.zeros((EXTRA, DIM + NV - BLK), jnp.bfloat16)
    q = proxies[...]
    qf = q.astype(jnp.float32)
    qnorm = jnp.sum(qf * qf, axis=1, keepdims=True)
    cross = dot_nt(q, p)
    far = jnp.exp((qnorm + norm[0:1, :] - 2.0 * cross) * (-2.0 / DIM))
    gram[...] = dot_nt(far, far, HIGH)


def factor_kernel(g0, s1, s2, out):
    zeros = jnp.zeros((RANK, RANK), jnp.float32)
    rows = lax.broadcasted_iota(jnp.int32, (RANK, 2 * RANK), 0)
    lanes = lax.broadcasted_iota(jnp.int32, (RANK, 2 * RANK), 1)
    eye = jnp.where(rows == lanes - RANK, 1.0, 0.0)
    gram0 = g0[...]
    gram1 = gram0 + s1[...]
    gram2 = gram1 + s2[...]
    work = []
    for g in (gram0, gram1, gram2):
        full = jnp.concatenate([g, zeros], axis=1) + eye
        work.append([full[8 * b : 8 * b + 8, :] for b in range(RANK // 8)])
    sub = lax.broadcasted_iota(jnp.int32, (8, 2 * RANK), 0)
    lane = lax.broadcasted_iota(jnp.int32, (8, 2 * RANK), 1)
    for k in range(RANK - 1):
        b0, s0 = divmod(k, 8)
        for m in range(3):
            w = work[m]
            row = w[b0][s0 : s0 + 1, :]
            row = row * (-1.0 / row[:, k : k + 1])
            for b in range(b0, RANK // 8):
                if b == b0:
                    if s0 == 7:
                        continue
                    col = jnp.where(sub > s0, w[b][:, k : k + 1], 0.0)
                else:
                    col = w[b][:, k : k + 1]
                w[b] = w[b] + col * row
    uppers, inverses = [], []
    for m in range(3):
        done = []
        for b in range(RANK // 8):
            w = work[m][b]
            diag = jnp.sum(jnp.where(lane == sub + 8 * b, w, 0.0), axis=1, keepdims=True)
            w = w * lax.rsqrt(diag)
            done.append(jnp.where((lane >= RANK) | (lane >= sub + 8 * b), w, 0.0))
        full = jnp.concatenate(done, axis=0)
        uppers.append(full[:, :RANK])
        inverses.append(full[:, RANK:])
    out[:, 0:RANK] = dot_nt(uppers[0], inverses[1], HIGH)
    out[:, RANK : 2 * RANK] = dot_nt(uppers[1], inverses[2], HIGH)
    out[:, 2 * RANK :] = uppers[2]


def near_kernel(ids, t01, t23, s01, s23, own, out1, out2, out3, bias):
    def target(k):
        return (t01, t23)[k // 2][(k % 2) * UNIT : (k % 2 + 1) * UNIT, :]

    def source(k, lo, hi, first, last):
        base = (k % 2) * ROWS
        return (s01, s23)[k // 2][base + lo : base + hi, first:last]

    rows = lax.broadcasted_iota(jnp.int32, (4 * NB, BLK), 0)
    lanes = lax.broadcasted_iota(jnp.int32, (4 * NB, BLK), 1)
    wanted = jnp.zeros((4 * NB, BLK), jnp.int32)
    for k in range(4):
        wanted = jnp.where(rows // NB == k, ids[k] * NB + rows % NB, wanted)
    pick = jnp.where(wanted == lanes, 1.0, 0.0).astype(jnp.bfloat16)
    for k in range(4):
        extra = source(k, UNIT, ROWS, 0, BLK)
        count = dot_nt(pick, extra)
        level = jnp.where(count > 0.5, jnp.log2(jnp.maximum(count, 1.0)), -1e30)
        parts = extra.astype(jnp.float32)
        for b in range(NB):
            norm = parts[NB + b : NB + b + 1] + parts[2 * NB + b : 2 * NB + b + 1] + parts[3 * NB + b : 3 * NB + b + 1]
            bias[:, k * UNIT + b * BLK : k * UNIT + (b + 1) * BLK] = (
                level[:, b : b + 1] - norm * (2.0 * LOG2E / DIM)
            )
    for t, out in ((3, out3), (2, out2), (1, out1), (0, own)):
        left = target(t)
        total = None
        for k in range(4):
            cross = dot_nt(left, source(k, 0, UNIT, 0, DIM))
            tiles = []
            for b in range(NB):
                i = t * NB + b
                row = bias[i : i + 1, k * UNIT : (k + 1) * UNIT]
                tiles.append(
                    jnp.exp2(cross[b * BLK : (b + 1) * BLK, :] * (4.0 * LOG2E / DIM) + row).astype(jnp.bfloat16)
                )
            tile = jnp.concatenate(tiles, axis=0)
            part = jnp.dot(tile, source(k, 0, UNIT, DIM, DIM + NV), preferred_element_type=jnp.float32)
            total = part if total is None else total + part
        out[...] = total.astype(out.dtype)


def finish_kernel(own, r1, r2, r3, scale, out):
    total = (
        own[...] + r1[...].astype(jnp.float32) + r2[...].astype(jnp.float32) + r3[...].astype(jnp.float32)
    )
    out[...] = (total * scale[...]).astype(jnp.bfloat16)


def call(kernel, shapes, *args, scratch=(), scalars=0, flops=0, nbytes=0):
    return pl.pallas_call(
        kernel,
        out_shape=shapes,
        in_specs=[pl.BlockSpec(memory_space=pltpu.SMEM)] * scalars
        + [pl.BlockSpec(memory_space=pltpu.VMEM)] * (len(args) - scalars),
        out_specs=jax.tree.map(lambda _: pl.BlockSpec(memory_space=pltpu.VMEM), shapes),
        scratch_shapes=list(scratch),
        compiler_params=pltpu.CompilerParams(vmem_limit_bytes=VMEM),
        cost_estimate=pl.CostEstimate(flops=flops, bytes_accessed=nbytes, transcendentals=0),
    )(*args)


def exchange(value, mask, first):
    n_col = lax.axis_size("col")
    pairs = []
    for y in range(SIDE):
        for x in range(SIDE):
            for c in range(n_col):
                along_x = c % 2 == first
                other = y * SIDE + (x ^ mask) if along_x else (y ^ mask) * SIDE + x
                pairs.append(((y * SIDE + x) * n_col + c, other * n_col + c))
    return lax.ppermute(value, ("row", "col"), pairs)


def partner(value, mask):
    return lax.ppermute(value, "col", [(c, c ^ mask) for c in range(lax.axis_size("col"))])


def on_device(points, weights, near_blocks, proxies):
    f32, bf16 = jnp.float32, jnp.bfloat16
    shape = jax.ShapeDtypeStruct
    send, gram, scale = call(
        prepare_kernel,
        (shape((ROWS, DIM + NV), bf16), shape((RANK, RANK), f32), shape((UNIT, NV), f32)),
        points,
        weights,
        near_blocks,
        proxies,
    )
    s1 = exchange(send, 1, 1)
    t1 = exchange(points, 3, 0)
    g1 = partner(gram, 1)
    s01 = jnp.concatenate([send, s1], axis=0)
    t01 = jnp.concatenate([points, t1], axis=0)
    s23 = exchange(s01, 3, 1)
    t23 = exchange(t01, 1, 0)
    g2 = partner(gram + g1, 2)
    factors = call(factor_kernel, shape((RANK, 3 * RANK), f32), gram, g1, g2)
    row = lax.axis_index("row")
    even = lax.axis_index("col") % 2 == 0
    ids = jnp.stack([jnp.where(even, row ^ m, row ^ (m * SIDE)) for m in (0, 3, 1, 2)]).astype(jnp.int32)
    own, p1, p2, p3 = call(
        near_kernel,
        (shape((UNIT, NV), f32),) + (shape((UNIT, NV), bf16),) * 3,
        ids,
        t01,
        t23,
        s01,
        s23,
        scratch=[pltpu.VMEM((4 * NB, 4 * UNIT), f32)],
        scalars=1,
    )
    r3 = exchange(p3, 2, 0)
    r2 = exchange(p2, 1, 0)
    r1 = exchange(p1, 3, 0)
    near_product = call(finish_kernel, shape((UNIT, NV), bf16), own, r1, r2, r3, scale)
    return (near_product, factors)


def solution(mesh):
    placed = (P(("col", "row"), None), P(("col", "row"), None), P(("col", "row"), None), P())
    return jax.shard_map(
        on_device,
        mesh=mesh,
        in_specs=placed,
        out_specs=(P(("col", "row"), None), P(("col", "row"), None)),
        check_vma=False,
    )
```

time: 214 us -> 68.8 us (0.32)
  the two profiles are of different devices: /device:TPU:2 before, /device:TPU:8 now
where the time goes in v1:
time: 68.8 us; the launch traced here: 68.4 us
  starting transfers between devices  27.8 us (40%)
  waiting for transfers between devices  22.4 us (33%)
  Pallas kernels  13.9 us (20%)
  local copies, waits for them, and re-layouts  3.43 us (5%)
  between operations  0.78 us (1%)
    ppermute x7, starting transfers between devices, exchange(): return lax.ppermute(value, ('row', 'col'), pairs)  23.9 us
    ppermute x7, waiting for transfers between devices, exchange(): return lax.ppermute(value, ('row', 'col'), pairs)  17.3 us
    pallas_call x4, Pallas kernels, call(): pl.pallas_call(kernel, out_shape=shapes, in_specs=[pl.BlockSpec(memory_sp...  13.9 us
    ppermute x2, waiting for transfers between devices, partner(): lax.ppermute(value, 'col', [(c, c ^ mask) for c in range(lax.axis_size('c...  5.05 us
    ppermute x2, starting transfers between devices, partner(): lax.ppermute(value, 'col', [(c, c ^ mask) for c in range(lax.axis_size('c...  3.83 us
    unnamed x10, local copies, waits for them, and re-layouts  3.35 us
  transfers between devices with their start and end apart: 9, of which 5 were waited for; matrix products, arithmetic and copies ran while one was open for 0% of the time, Pallas kernels for 10%

profile of v1, /device:TPU:8, one launch (start us, length us, event | category | flops | bytes accessed | tf_op | source)
XLA Modules:
  0.0 68.4 jit_solution(9544882976189243138)
XLA Ops:
  0.6 0.0 copy-start
  0.6 0.9 %copy-done = bf16[512,256]{1,0:T(8,128)(2,1)S(1)} copy-done((bf16[512,256]{1,0:T(8,128)(2,1)S(1)}, bf16[512,256]{1,0:T(8,128)(2,1)}, u32[]{:S(2)}) %copy-start) | copy-done | bytes 262168
  1.6 0.0 copy-start.1
  1.6 0.9 %copy-done.1 = bf16[512,128]{1,0:T(8,128)(2,1)S(1)} copy-done((bf16[512,128]{1,0:T(8,128)(2,1)S(1)}, bf16[512,128]{1,0:T(8,128)(2,1)}, u32[]{:S(2)}) %copy-start.1) | copy-done | bytes 131096
  2.5 0.0 copy-start.2
  2.5 0.8 %copy-done.2 = bf16[64,256]{1,0:T(8,128)(2,1)S(1)} copy-done((bf16[64,256]{1,0:T(8,128)(2,1)S(1)}, bf16[64,256]{1,0:T(8,128)(2,1)}, u32[]{:S(2)}) %copy-start.2) | copy-done | bytes 32792
  3.2 0.0 copy-start.3
  3.2 0.7 copy-done.3
  3.9 1.0 %shard_map.59 = (bf16[528,384]{1,0:T(8,128)(2,1)S(1)}, f32[64,64]{1,0:T(8,128)S(1)}, f32[512,128]{1,0:T(8,128)S(1)}) custom-call(bf16[512,256]{1,0:T(8,128)(2,1)S(1)} %copy-done, bf16[512,128]{1,0:T(8,128)(2,1)S(1)} %copy-done.1, s32[4,16]{1,0:T(4,128)S(1)} %copy-done.3, bf16[64,256]{1,0:T(8,128)(2,1)S(1)} %copy-done.2), custom_call_target="tpu_custom_call" | custom-call | tf_op jit(solution)/shard_map/pallas_call | solution.py:164
  4.9 7.7 %collective-permute-start.2 = (bf16[528,384]{1,0:T(8,128)(2,1)S(1)}, bf16[528,384]{1,0:T(8,128)(2,1)S(1)}, u32[]{:S(2)}, u32[]{:S(2)}) collective-permute-start(bf16[528,384]{1,0:T(8,128)(2,1)S(1)} %get-tuple-element.9), channel_id=1, source_target_pairs={{0,128},{1,33},{2,130},{3,35},{4,132},{5,37},{6,134},{7,39},{8,136... | collective-permute-start | bytes 1216520 | tf_op jit(solution)/shard_map/ppermute | solution.py:185
  12.6 1.9 %collective-permute-start = (bf16[512,256]{1,0:T(8,128)(2,1)S(1)}, bf16[512,256]{1,0:T(8,128)(2,1)S(1)}, u32[]{:S(2)}, u32[]{:S(2)}) collective-permute-start(bf16[512,256]{1,0:T(8,128)(2,1)S(1)} %copy-done), channel_id=1, source_target_pairs={{0,96},{1,385},{2,98},{3,387},{4,100},{5,389},{6,102},{7,391},{8,1... | collective-permute-start | bytes 786440 | tf_op jit(solution)/shard_map/ppermute | solution.py:185
  14.6 3.9 %collective-permute-done.2 = bf16[528,384]{1,0:T(8,128)(2,1)S(1)} collective-permute-done((bf16[528,384]{1,0:T(8,128)(2,1)S(1)}, bf16[528,384]{1,0:T(8,128)(2,1)S(1)}, u32[]{:S(2)}, u32[]{:S(2)}) %collective-permute-start.2) | collective-permute-done | bytes 405536 | tf_op jit(solution)/shard_map/ppermute | solution.py:185
  18.5 0.1 constant_dynamic-update-slice_fusion.2.s01
  18.6 1.9 %collective-permute-start.3 = (bf16[1056,384]{1,0:T(8,128)(2,1)S(1)}, bf16[1056,384]{1,0:T(8,128)(2,1)S(1)}, u32[]{:S(2)}, u32[]{:S(2)}) collective-permute-start(bf16[1056,384]{1,0:T(8,128)(2,1)S(1)} %constant_dynamic-update-slice_fusion.2.s01), channel_id=1, source_target_pairs={{0,384},{1,97},{2,386},{3,99},{4,388},{5,101},{6,390},{7,103},{8,3... | collective-permute-start | bytes 2433032 | tf_op jit(solution)/shard_map/ppermute | solution.py:185
  20.5 4.4 %collective-permute-done = bf16[512,256]{1,0:T(8,128)(2,1)S(1)} collective-permute-done((bf16[512,256]{1,0:T(8,128)(2,1)S(1)}, bf16[512,256]{1,0:T(8,128)(2,1)S(1)}, u32[]{:S(2)}, u32[]{:S(2)}) %collective-permute-start) | collective-permute-done | bytes 262176 | tf_op jit(solution)/shard_map/ppermute | solution.py:185
  24.9 1.9 %collective-permute-start.1 = (bf16[1024,256]{1,0:T(8,128)(2,1)S(1)}, bf16[1024,256]{1,0:T(8,128)(2,1)S(1)}, u32[]{:S(2)}, u32[]{:S(2)}) collective-permute-start(bf16[1024,256]{1,0:T(8,128)(2,1)S(1)} %constant_dynamic-update-slice_fusion.t01), channel_id=1, source_target_pairs={{0,32},{1,129},{2,34},{3,131},{4,36},{5,133},{6,38},{7,135},{8,40}... | collective-permute-start | bytes 1572872 | tf_op jit(solution)/shard_map/ppermute | solution.py:185
  26.9 0.1 pad_add_fusion.ids
  27.0 9.0 %collective-permute-done.1.t23 = bf16[1024,256]{1,0:T(8,128)(2,1)S(1)} collective-permute-done((bf16[1024,256]{1,0:T(8,128)(2,1)S(1)}, bf16[1024,256]{1,0:T(8,128)(2,1)S(1)}, u32[]{:S(2)}, u32[]{:S(2)}) %collective-permute-start.1) | collective-permute-done | bytes 524320 | tf_op jit(solution)/shard_map/ppermute | solution.py:185
  36.0 0.0 collective-permute-done.3.s23
  36.0 5.6 %shard_map.60 = (f32[512,128]{1,0:T(8,128)S(1)}, bf16[512,128]{1,0:T(8,128)(2,1)S(1)}, bf16[512,128]{1,0:T(8,128)(2,1)S(1)}, bf16[512,128]{1,0:T(8,128)(2,1)S(1)}) custom-call(s32[4]{0:T(128)S(1)} %pad_add_fusion.ids, bf16[1024,256]{1,0:T(8,128)(2,1)S(1)} %constant_dynamic-update-slice_fusion.t01, bf16[1024,256]{1,0:T(8,128)(2,1)S(1)} %collective-permute-done.1.t23, ...), custom_call_target="tpu_custom_call" | custom-call | tf_op jit(solution)/shard_map/pallas_call | solution.py:164
  41.6 1.9 %collective-permute-start.4 = (bf16[512,128]{1,0:T(8,128)(2,1)S(1)}, bf16[512,128]{1,0:T(8,128)(2,1)S(1)}, u32[]{:S(2)}, u32[]{:S(2)}) collective-permute-start(bf16[512,128]{1,0:T(8,128)(2,1)S(1)} %get-tuple-element.11), channel_id=1, source_target_pairs={{0,96},{1,385},{2,98},{3,387},{4,100},{5,389},{6,102},{7,391},{8,1... | collective-permute-start | bytes 393224 | tf_op jit(solution)/shard_map/ppermute | solution.py:185
  43.6 1.9 %collective-permute-start.5 = (bf16[512,128]{1,0:T(8,128)(2,1)S(1)}, bf16[512,128]{1,0:T(8,128)(2,1)S(1)}, u32[]{:S(2)}, u32[]{:S(2)}) collective-permute-start(bf16[512,128]{1,0:T(8,128)(2,1)S(1)} %get-tuple-element.12), channel_id=1, source_target_pairs={{0,32},{1,129},{2,34},{3,131},{4,36},{5,133},{6,38},{7,135},{8,40}... | collective-permute-start | bytes 393224 | tf_op jit(solution)/shard_map/ppermute | solution.py:185
  45.5 6.6 %collective-permute-start.6 = (bf16[512,128]{1,0:T(8,128)(2,1)S(1)}, bf16[512,128]{1,0:T(8,128)(2,1)S(1)}, u32[]{:S(2)}, u32[]{:S(2)}) collective-permute-start(bf16[512,128]{1,0:T(8,128)(2,1)S(1)} %get-tuple-element.13), channel_id=1, source_target_pairs={{0,64},{1,257},{2,66},{3,259},{4,68},{5,261},{6,70},{7,263},{8,72}... | collective-permute-start | bytes 393224 | tf_op jit(solution)/shard_map/ppermute | solution.py:185
  52.1 1.9 %collective-permute-start.7 = (f32[64,64]{1,0:T(8,128)S(1)}, f32[64,64]{1,0:T(8,128)S(1)}, u32[]{:S(2)}, u32[]{:S(2)}) collective-permute-start(f32[64,64]{1,0:T(8,128)S(1)} %get-tuple-element.15.g0), channel_id=1, source_target_pairs={{0,1},{1,0},{2,3},{3,2},{4,5},{5,4},{6,7},{7,6},{8,9},{9,8},{10,11... | collective-permute-start | bytes 49160 | tf_op jit(solution)/shard_map/ppermute | solution.py:189
  54.0 1.2 %collective-permute-done.7.s1 = f32[64,64]{1,0:T(8,128)S(1)} collective-permute-done((f32[64,64]{1,0:T(8,128)S(1)}, f32[64,64]{1,0:T(8,128)S(1)}, u32[]{:S(2)}, u32[]{:S(2)}) %collective-permute-start.7) | collective-permute-done | bytes 16416 | tf_op jit(solution)/shard_map/ppermute | solution.py:189
  55.2 1.9 %collective-permute-start.8 = (f32[64,64]{1,0:T(8,128)S(1)}, f32[64,64]{1,0:T(8,128)S(1)}, u32[]{:S(2)}, u32[]{:S(2)}) collective-permute-start(f32[64,64]{1,0:T(8,128)S(1)} %add.8), channel_id=1, source_target_pairs={{0,2},{1,3},{2,0},{3,1},{4,6},{5,7},{6,4},{7,5},{8,10},{9,11},{10,... | collective-permute-start | bytes 49160 | tf_op jit(solution)/shard_map/ppermute | solution.py:189
  57.1 3.9 %collective-permute-done.8.s2 = f32[64,64]{1,0:T(8,128)S(1)} collective-permute-done((f32[64,64]{1,0:T(8,128)S(1)}, f32[64,64]{1,0:T(8,128)S(1)}, u32[]{:S(2)}, u32[]{:S(2)}) %collective-permute-start.8) | collective-permute-done | bytes 16416 | tf_op jit(solution)/shard_map/ppermute | solution.py:189
  61.0 6.6 %shard_map.62 = f32[64,192]{1,0:T(8,128)} custom-call(f32[64,64]{1,0:T(8,128)S(1)} %get-tuple-element.15.g0, f32[64,64]{1,0:T(8,128)S(1)} %collective-permute-done.7.s1, f32[64,64]{1,0:T(8,128)S(1)} %collective-permute-done.8.s2), custom_call_target="tpu_custom_call" | custom-call | tf_op jit(solution)/shard_map/pallas_call | solution.py:164
  67.6 0.0 collective-permute-done.4.r1
  67.6 0.0 collective-permute-done.5.r2
  67.6 0.0 collective-permute-done.6.r3
  67.6 0.7 %shard_map.61 = bf16[512,128]{1,0:T(8,128)(2,1)} custom-call(f32[512,128]{1,0:T(8,128)S(1)} %get-tuple-element.10.own, bf16[512,128]{1,0:T(8,128)(2,1)S(1)} %collective-permute-done.4.r1, bf16[512,128]{1,0:T(8,128)(2,1)S(1)} %collective-permute-done.5.r2, bf16[512,128]{1,0:T(8,128)(2,1)S(1)} %collective-permute-done.6.r3, f32[512,128]{1,0:T(8,128)S(1)} %get-tuple-element.14.scale), custom_call_target="tpu_custom_call" | custom-call | tf_op jit(solution)/shard_map/pallas_call | solution.py:164
  (4 shorter events, 0.1 us)
Async XLA Ops:
  0.6 1.0 %copy-start = (bf16[512,256]{1,0:T(8,128)(2,1)S(1)}, bf16[512,256]{1,0:T(8,128)(2,1)}, u32[]{:S(2)}) copy-start(bf16[512,256]{1,0:T(8,128)(2,1)} %points.1) | copy-start | bytes 786436
  1.6 0.9 %copy-start.1 = (bf16[512,128]{1,0:T(8,128)(2,1)S(1)}, bf16[512,128]{1,0:T(8,128)(2,1)}, u32[]{:S(2)}) copy-start(bf16[512,128]{1,0:T(8,128)(2,1)} %weights.1) | copy-start | bytes 393220
  2.5 0.8 %copy-start.2 = (bf16[64,256]{1,0:T(8,128)(2,1)S(1)}, bf16[64,256]{1,0:T(8,128)(2,1)}, u32[]{:S(2)}) copy-start(bf16[64,256]{1,0:T(8,128)(2,1)} %proxies.1) | copy-start | bytes 98308
  3.2 0.7 copy-start.3
  4.9 13.6 %collective-permute-start.2 = (bf16[528,384]{1,0:T(8,128)(2,1)S(1)}, bf16[528,384]{1,0:T(8,128)(2,1)S(1)}, u32[]{:S(2)}, u32[]{:S(2)}) collective-permute-start(bf16[528,384]{1,0:T(8,128)(2,1)S(1)} %get-tuple-element.9), channel_id=1, source_target_pairs={{0,128},{1,33},{2,130},{3,35},{4,132},{5,37},{6,134},{7,39},{8,136... | collective-permute-start | bytes 1216520 | tf_op jit(solution)/shard_map/ppermute | solution.py:185
  12.6 12.3 %collective-permute-start = (bf16[512,256]{1,0:T(8,128)(2,1)S(1)}, bf16[512,256]{1,0:T(8,128)(2,1)S(1)}, u32[]{:S(2)}, u32[]{:S(2)}) collective-permute-start(bf16[512,256]{1,0:T(8,128)(2,1)S(1)} %copy-done), channel_id=1, source_target_pairs={{0,96},{1,385},{2,98},{3,387},{4,100},{5,389},{6,102},{7,391},{8,1... | collective-permute-start | bytes 786440 | tf_op jit(solution)/shard_map/ppermute | solution.py:185
  18.6 17.4 %collective-permute-start.3 = (bf16[1056,384]{1,0:T(8,128)(2,1)S(1)}, bf16[1056,384]{1,0:T(8,128)(2,1)S(1)}, u32[]{:S(2)}, u32[]{:S(2)}) collective-permute-start(bf16[1056,384]{1,0:T(8,128)(2,1)S(1)} %constant_dynamic-update-slice_fusion.2.s01), channel_id=1, source_target_pairs={{0,384},{1,97},{2,386},{3,99},{4,388},{5,101},{6,390},{7,103},{8,3... | collective-permute-start | bytes 2433032 | tf_op jit(solution)/shard_map/ppermute | solution.py:185
  24.9 11.1 %collective-permute-start.1 = (bf16[1024,256]{1,0:T(8,128)(2,1)S(1)}, bf16[1024,256]{1,0:T(8,128)(2,1)S(1)}, u32[]{:S(2)}, u32[]{:S(2)}) collective-permute-start(bf16[1024,256]{1,0:T(8,128)(2,1)S(1)} %constant_dynamic-update-slice_fusion.t01), channel_id=1, source_target_pairs={{0,32},{1,129},{2,34},{3,131},{4,36},{5,133},{6,38},{7,135},{8,40}... | collective-permute-start | bytes 1572872 | tf_op jit(solution)/shard_map/ppermute | solution.py:185
  41.6 26.0 %collective-permute-start.4 = (bf16[512,128]{1,0:T(8,128)(2,1)S(1)}, bf16[512,128]{1,0:T(8,128)(2,1)S(1)}, u32[]{:S(2)}, u32[]{:S(2)}) collective-permute-start(bf16[512,128]{1,0:T(8,128)(2,1)S(1)} %get-tuple-element.11), channel_id=1, source_target_pairs={{0,96},{1,385},{2,98},{3,387},{4,100},{5,389},{6,102},{7,391},{8,1... | collective-permute-start | bytes 393224 | tf_op jit(solution)/shard_map/ppermute | solution.py:185
  43.6 24.1 %collective-permute-start.5 = (bf16[512,128]{1,0:T(8,128)(2,1)S(1)}, bf16[512,128]{1,0:T(8,128)(2,1)S(1)}, u32[]{:S(2)}, u32[]{:S(2)}) collective-permute-start(bf16[512,128]{1,0:T(8,128)(2,1)S(1)} %get-tuple-element.12), channel_id=1, source_target_pairs={{0,32},{1,129},{2,34},{3,131},{4,36},{5,133},{6,38},{7,135},{8,40}... | collective-permute-start | bytes 393224 | tf_op jit(solution)/shard_map/ppermute | solution.py:185
  45.5 22.1 %collective-permute-start.6 = (bf16[512,128]{1,0:T(8,128)(2,1)S(1)}, bf16[512,128]{1,0:T(8,128)(2,1)S(1)}, u32[]{:S(2)}, u32[]{:S(2)}) collective-permute-start(bf16[512,128]{1,0:T(8,128)(2,1)S(1)} %get-tuple-element.13), channel_id=1, source_target_pairs={{0,64},{1,257},{2,66},{3,259},{4,68},{5,261},{6,70},{7,263},{8,72}... | collective-permute-start | bytes 393224 | tf_op jit(solution)/shard_map/ppermute | solution.py:185
  52.1 3.1 %collective-permute-start.7 = (f32[64,64]{1,0:T(8,128)S(1)}, f32[64,64]{1,0:T(8,128)S(1)}, u32[]{:S(2)}, u32[]{:S(2)}) collective-permute-start(f32[64,64]{1,0:T(8,128)S(1)} %get-tuple-element.15.g0), channel_id=1, source_target_pairs={{0,1},{1,0},{2,3},{3,2},{4,5},{5,4},{6,7},{7,6},{8,9},{9,8},{10,11... | collective-permute-start | bytes 49160 | tf_op jit(solution)/shard_map/ppermute | solution.py:189
  55.2 5.8 %collective-permute-start.8 = (f32[64,64]{1,0:T(8,128)S(1)}, f32[64,64]{1,0:T(8,128)S(1)}, u32[]{:S(2)}, u32[]{:S(2)}) collective-permute-start(f32[64,64]{1,0:T(8,128)S(1)} %add.8), channel_id=1, source_target_pairs={{0,2},{1,3},{2,0},{3,1},{4,6},{5,7},{6,4},{7,5},{8,10},{9,11},{10,... | collective-permute-start | bytes 49160 | tf_op jit(solution)/shard_map/ppermute | solution.py:189

commit v2 on v1

v2 whole, which is shorter than its diff:
```python
import functools

import jax
import jax.numpy as jnp
import numpy as np
from jax import lax
from jax.experimental import pallas as pl
from jax.experimental.pallas import tpu as pltpu
from jax.sharding import PartitionSpec as P

DIM = 256
RANK = 64
BLK = 128
NV = 128
UNIT = 512
NB = 4
SIDE = 4
EXTRA = 16
ROWS = UNIT + EXTRA
GROUP = 64
LOG2E = 1.4426950408889634
LINE = 4
PANEL = 4
NT = (((1,), (1,)), ((), ()))
HIGH = lax.Precision.HIGHEST
VMEM = 24 * 1024 * 1024
SEND_VMEM = 62 * 1024 * 1024


def dot_nt(a, b, precision=None):
    return lax.dot_general(a, b, NT, precision=precision, preferred_element_type=jnp.float32)


def split2(x):
    hi = x.astype(jnp.bfloat16)
    return hi, (x - hi.astype(jnp.float32)).astype(jnp.bfloat16)


def row_norms(squares):
    hi, lo = squares
    ones = jnp.ones((8, DIM), jnp.bfloat16)
    return dot_nt(ones, hi) + dot_nt(ones, lo)


def send_kernel(points, weights, near, send, ids, sems):
    copies = [
        pltpu.make_async_copy(points, send.at[pl.ds(0, UNIT), pl.ds(0, DIM)], sems.at[0]),
        pltpu.make_async_copy(near, ids, sems.at[1]),
        pltpu.make_async_copy(weights, send.at[pl.ds(0, UNIT), pl.ds(DIM, NV)], sems.at[2]),
    ]
    for copy in copies:
        copy.start()
    send[UNIT:, BLK:] = jnp.zeros((EXTRA, DIM + NV - BLK), jnp.bfloat16)
    copies[1].wait()
    local = ids[...] & (GROUP - 1)
    lanes = lax.broadcasted_iota(jnp.int32, (NB, BLK), 1)
    counts = jnp.zeros((NB, BLK), jnp.float32)
    for t in range(near.shape[1]):
        counts = counts + jnp.where(local[:, t : t + 1] == lanes, 1.0, 0.0)
    copies[0].wait()
    f = send[:UNIT, :DIM].astype(jnp.float32)
    norm = row_norms(split2(f * f))
    rows = jnp.concatenate([norm[0:1, b * BLK : (b + 1) * BLK] for b in range(NB)], axis=0)
    first = rows.astype(jnp.bfloat16).astype(jnp.float32)
    second = (rows - first).astype(jnp.bfloat16).astype(jnp.float32)
    third = rows - first - second
    extra = jnp.concatenate([counts, first, second, third], axis=0)
    send[UNIT:, :BLK] = extra.astype(jnp.bfloat16)
    copies[2].wait()


def gram_kernel(send, proxies, gram, scale):
    p = send[:UNIT, :DIM]
    f = p.astype(jnp.float32)
    squares = split2(f * f)
    tall = jnp.ones((DIM, NV), jnp.bfloat16)
    column = jnp.dot(squares[0], tall, preferred_element_type=jnp.float32) + jnp.dot(
        squares[1], tall, preferred_element_type=jnp.float32
    )
    scale[...] = jnp.exp(column * (-2.0 / DIM))
    q = proxies[...]
    qf = q.astype(jnp.float32)
    qnorm = jnp.sum(qf * qf, axis=1, keepdims=True)
    far = jnp.exp((qnorm + row_norms(squares)[0:1, :] - 2.0 * dot_nt(q, p)) * (-2.0 / DIM))
    gram[...] = dot_nt(far, far, HIGH)


def factor_kernel(g0, s1, s2, out):
    zeros = jnp.zeros((RANK, RANK), jnp.float32)
    rows = lax.broadcasted_iota(jnp.int32, (RANK, 2 * RANK), 0)
    lanes = lax.broadcasted_iota(jnp.int32, (RANK, 2 * RANK), 1)
    eye = jnp.where(rows == lanes - RANK, 1.0, 0.0)
    gram0 = g0[...]
    gram1 = gram0 + s1[...]
    gram2 = gram1 + s2[...]
    work = []
    for g in (gram0, gram1, gram2):
        full = jnp.concatenate([g, zeros], axis=1) + eye
        work.append([full[8 * b : 8 * b + 8, :] for b in range(RANK // 8)])
    sub = lax.broadcasted_iota(jnp.int32, (8, 2 * RANK), 0)
    lane = lax.broadcasted_iota(jnp.int32, (8, 2 * RANK), 1)
    for k0 in range(0, RANK, PANEL):
        b0 = k0 // 8
        cols = [
            [
                {b: jnp.broadcast_to(w[b][:, k : k + 1], (8, 2 * RANK)) for b in range(b0, RANK // 8)}
                for k in range(k0, k0 + PANEL)
            ]
            for w in work
        ]
        for j in range(PANEL):
            s0 = (k0 + j) % 8
            for w, c in zip(work, cols):
                inverse = -1.0 / c[j][b0][s0 : s0 + 1, :]
                row = w[b0][s0 : s0 + 1, :] * inverse
                later = [c[i][b0][s0 : s0 + 1, :] * inverse for i in range(j + 1, PANEL)]
                for b in range(b0, RANK // 8):
                    col = c[j][b]
                    if b == b0:
                        if s0 == 7:
                            continue
                        col = jnp.where(sub > s0, col, 0.0)
                    w[b] = w[b] + col * row
                    for i, entry in enumerate(later, j + 1):
                        c[i][b] = c[i][b] + col * entry
    uppers, inverses = [], []
    for m in range(3):
        done = []
        for b in range(RANK // 8):
            w = work[m][b]
            diag = jnp.sum(jnp.where(lane == sub + 8 * b, w, 0.0), axis=1, keepdims=True)
            w = w * lax.rsqrt(diag)
            done.append(jnp.where((lane >= RANK) | (lane >= sub + 8 * b), w, 0.0))
        full = jnp.concatenate(done, axis=0)
        uppers.append(full[:, :RANK])
        inverses.append(full[:, RANK:])
    out[:, 0:RANK] = dot_nt(uppers[0], inverses[1], HIGH)
    out[:, RANK : 2 * RANK] = dot_nt(uppers[1], inverses[2], HIGH)
    out[:, 2 * RANK :] = uppers[2]


def bias_rows(ids, sources, bias):
    rows = lax.broadcasted_iota(jnp.int32, (LINE * NB, BLK), 0)
    lanes = lax.broadcasted_iota(jnp.int32, (LINE * NB, BLK), 1)
    wanted = jnp.zeros((LINE * NB, BLK), jnp.int32)
    for k in range(LINE):
        wanted = jnp.where(rows // NB == k, ids[k] * NB + rows % NB, wanted)
    pick = jnp.where(wanted == lanes, 1.0, 0.0).astype(jnp.bfloat16)
    for k, source in enumerate(sources):
        extra = source[UNIT:ROWS, :BLK]
        count = dot_nt(pick, extra)
        level = jnp.where(count > 0.5, jnp.log2(jnp.maximum(count, 1.0)), -1e30)
        parts = extra.astype(jnp.float32)
        for b in range(NB):
            norm = parts[NB + b : NB + b + 1] + parts[2 * NB + b : 2 * NB + b + 1] + parts[3 * NB + b : 3 * NB + b + 1]
            bias[:, k * UNIT + b * BLK : k * UNIT + (b + 1) * BLK] = (
                level[:, b : b + 1] - norm * (2.0 * LOG2E / DIM)
            )


def near_sum(left, t, sources, bias, total=None):
    for k, source in enumerate(sources):
        cross = dot_nt(left, source[:UNIT, :DIM])
        tiles = []
        for b in range(NB):
            i = t * NB + b
            row = bias[i : i + 1, k * UNIT : (k + 1) * UNIT]
            tiles.append(
                jnp.exp2(cross[b * BLK : (b + 1) * BLK, :] * (4.0 * LOG2E / DIM) + row).astype(jnp.bfloat16)
            )
        tile = jnp.concatenate(tiles, axis=0)
        part = jnp.dot(tile, source[:UNIT, DIM:], preferred_element_type=jnp.float32)
        total = part if total is None else total + part
    return total


def near_first_kernel(ids, s0, s1, t1, own, other, bias):
    bias_rows(ids, (s0, s1), bias)
    own[...] = near_sum(s0[:UNIT, :DIM], 0, (s0, s1), bias)
    other[...] = near_sum(t1[...], 1, (s0, s1), bias)


def near_out_kernel(ids, s0, s1, s2, s3, t1, t23, other, bias01, out, bias):
    bias_rows(ids, (s2, s3), bias)
    total = near_sum(t23[UNIT:, :], 3, (s0, s1), bias01)
    out[UNIT:, :] = near_sum(t23[UNIT:, :], 3, (s2, s3), bias, total).astype(jnp.bfloat16)
    out[:UNIT, :] = near_sum(t1[...], 1, (s2, s3), bias, other[...]).astype(jnp.bfloat16)


def near_in_kernel(s0, s1, s2, s3, t23, own, bias01, bias, own_out, out):
    total = near_sum(t23[:UNIT, :], 2, (s0, s1), bias01)
    out[...] = near_sum(t23[:UNIT, :], 2, (s2, s3), bias, total)
    own_out[...] = near_sum(s0[:UNIT, :DIM], 0, (s2, s3), bias, own[...])


def relay_kernel(mine, received, out):
    out[...] = (mine[...] + received[UNIT:, :].astype(jnp.float32)).astype(jnp.bfloat16)


def finish_kernel(own, first, second, scale, out):
    total = own[...] + first[:UNIT, :].astype(jnp.float32) + second[...].astype(jnp.float32)
    out[...] = (total * scale[...]).astype(jnp.bfloat16)


def call(kernel, shapes, *args, scratch=(), scalars=0, space=pltpu.VMEM, vmem=VMEM):
    return pl.pallas_call(
        kernel,
        out_shape=shapes,
        in_specs=[pl.BlockSpec(memory_space=pltpu.SMEM)] * scalars
        + [pl.BlockSpec(memory_space=space)] * (len(args) - scalars),
        out_specs=jax.tree.map(lambda _: pl.BlockSpec(memory_space=pltpu.VMEM), shapes),
        scratch_shapes=list(scratch),
        compiler_params=pltpu.CompilerParams(vmem_limit_bytes=vmem),
    )(*args)


def exchange(value, mask, first):
    n_col = lax.axis_size("col")
    pairs = []
    for y in range(SIDE):
        for x in range(SIDE):
            for c in range(n_col):
                along_x = c % 2 == first
                other = y * SIDE + (x ^ mask) if along_x else (y ^ mask) * SIDE + x
                pairs.append(((y * SIDE + x) * n_col + c, other * n_col + c))
    return lax.ppermute(value, ("row", "col"), pairs)


def partner(value, mask):
    return lax.ppermute(value, "col", [(c, c ^ mask) for c in range(lax.axis_size("col"))])


def on_device(points, weights, near_blocks, proxies):
    f32, bf16 = jnp.float32, jnp.bfloat16
    shape = jax.ShapeDtypeStruct
    t1 = exchange(points, 1, 0)
    send = call(
        send_kernel,
        shape((ROWS, DIM + NV), bf16),
        points,
        weights,
        near_blocks,
        scratch=[pltpu.VMEM(near_blocks.shape, jnp.int32), pltpu.SemaphoreType.DMA((3,))],
        space=pltpu.HBM,
        vmem=SEND_VMEM,
    )
    s1 = exchange(send, 3, 1)
    s2 = exchange(send, 1, 1)
    t23 = exchange(jnp.concatenate([points, t1], axis=0), 3, 0)
    proxies, t1 = lax.optimization_barrier((proxies, t1))
    gram, scale = call(gram_kernel, (shape((RANK, RANK), f32), shape((UNIT, NV), f32)), send, proxies)
    s3 = exchange(s1, 1, 1)
    gram, s1 = lax.optimization_barrier((gram, s1))
    g1 = partner(gram, 1)
    row = lax.axis_index("row")
    odd = lax.axis_index("col") % 2
    ids = jnp.stack([jnp.where(odd == 1, row ^ (m * SIDE), row ^ m) for m in (0, 1, 3, 2)]).astype(jnp.int32)
    half = shape((LINE * NB, 2 * UNIT), f32)
    unit = shape((UNIT, NV), f32)
    own, other, bias01 = call(near_first_kernel, (unit, unit, half), ids, send, s1, t1, scalars=1)
    level1, later_ids = lax.optimization_barrier((gram + g1, ids))
    g2 = partner(level1, 2)
    out, bias23 = call(
        near_out_kernel,
        (shape((2 * UNIT, NV), bf16), half),
        later_ids,
        send,
        s1,
        s2,
        s3,
        t1,
        t23,
        other,
        bias01,
        scalars=1,
    )
    r1 = exchange(out, 1, 0)
    own, mine = call(near_in_kernel, (unit, unit), send, s1, s2, s3, t23, own, bias01, bias23)
    mine, g2 = lax.optimization_barrier((mine, g2))
    relayed = call(relay_kernel, shape((UNIT, NV), bf16), mine, r1)
    r2 = exchange(relayed, 3, 0)
    gram, own = lax.optimization_barrier((gram, own))
    factors = call(factor_kernel, shape((RANK, 3 * RANK), f32), gram, g1, g2)
    near_product = call(finish_kernel, shape((UNIT, NV), bf16), own, r1, r2, scale)
    return (near_product, factors)


def solution(mesh):
    placed = (P(("col", "row"), None), P(("col", "row"), None), P(("col", "row"), None), P())
    return jax.shard_map(
        on_device,
        mesh=mesh,
        in_specs=placed,
        out_specs=(P(("col", "row"), None), P(("col", "row"), None)),
        check_vma=False,
    )
```

time: 68.8 us -> 54.6 us (0.79)
  the two profiles are of different devices: /device:TPU:8 before, /device:TPU:2 now
where the time goes in v2:
time: 54.6 us; the launch traced here: 54.2 us
  starting transfers between devices  24.9 us (46%)
  waiting for transfers between devices  14.3 us (26%)
  Pallas kernels  14 us (26%)
  between operations  0.83 us (2%)
    ppermute x7, starting transfers between devices, exchange(): return lax.ppermute(value, ('row', 'col'), pairs)  21.1 us
    pallas_call x8, Pallas kernels, call(): pl.pallas_call(kernel, out_shape=shapes, in_specs=[pl.BlockSpec(memory_sp...  14 us
    ppermute x7, waiting for transfers between devices, exchange(): return lax.ppermute(value, ('row', 'col'), pairs)  12.5 us
    ppermute x2, starting transfers between devices, partner(): lax.ppermute(value, 'col', [(c, c ^ mask) for c in range(lax.axis_size('c...  3.85 us
    ppermute x2, waiting for transfers between devices, partner(): lax.ppermute(value, 'col', [(c, c ^ mask) for c in range(lax.axis_size('c...  1.77 us
  transfers between devices with their start and end apart: 9, of which 5 were waited for; matrix products, arithmetic and copies ran while one was open for 0% of the time, Pallas kernels for 19%

profile of v2, /device:TPU:2, one launch (start us, length us, event | category | flops | bytes accessed | tf_op | source)
XLA Modules:
  0.0 54.2 jit_solution(15990332263622027341)
XLA Ops:
  0.6 0.0 copy-start.2
  0.6 7.9 %collective-permute-start = (bf16[512,256]{1,0:T(8,128)(2,1)}, bf16[512,256]{1,0:T(8,128)(2,1)S(1)}, u32[]{:S(2)}, u32[]{:S(2)}) collective-permute-start(bf16[512,256]{1,0:T(8,128)(2,1)} %points.1), channel_id=1, source_target_pairs={{0,32},{1,129},{2,34},{3,131},{4,36},{5,133},{6,38},{7,135},{8,40}... | collective-permute-start | bytes 786440 | tf_op jit(solution)/shard_map/ppermute | solution.py:226
  8.6 2.0 %shard_map.59.send.s0 = bf16[528,384]{1,0:T(8,128)(2,1)} custom-call(bf16[512,256]{1,0:T(8,128)(2,1)} %points.1, bf16[512,128]{1,0:T(8,128)(2,1)} %weights.1, s32[4,16]{1,0:T(4,128)} %near.1), custom_call_target="tpu_custom_call" | custom-call | tf_op jit(solution)/shard_map/pallas_call | solution.py:206
  10.6 0.0 copy-start
  10.6 2.1 %collective-permute-start.1 = (bf16[528,384]{1,0:T(8,128)(2,1)}, bf16[528,384]{1,0:T(8,128)(2,1)S(1)}, u32[]{:S(2)}, u32[]{:S(2)}) collective-permute-start(bf16[528,384]{1,0:T(8,128)(2,1)} %shard_map.59.send.s0), channel_id=1, source_target_pairs={{0,384},{1,97},{2,386},{3,99},{4,388},{5,101},{6,390},{7,103},{8,3... | collective-permute-start | bytes 1216520 | tf_op jit(solution)/shard_map/ppermute | solution.py:226
  12.7 0.5 collective-permute-done.t1
  13.1 0.0 copy-done.2
  13.2 0.0 copy-start.1
  13.2 1.9 %collective-permute-start.4 = (bf16[1024,256]{1,0:T(8,128)(2,1)S(1)}, bf16[1024,256]{1,0:T(8,128)(2,1)S(1)}, u32[]{:S(2)}, u32[]{:S(2)}) collective-permute-start(bf16[1024,256]{1,0:T(8,128)(2,1)S(1)} %pad_maximum_fusion), channel_id=1, source_target_pairs={{0,96},{1,385},{2,98},{3,387},{4,100},{5,389},{6,102},{7,391},{8,1... | collective-permute-start | bytes 1572872 | tf_op jit(solution)/shard_map/ppermute | solution.py:226
  15.1 0.0 copy-done
  15.1 1.9 %collective-permute-start.2 = (bf16[528,384]{1,0:T(8,128)(2,1)S(1)}, bf16[528,384]{1,0:T(8,128)(2,1)S(1)}, u32[]{:S(2)}, u32[]{:S(2)}) collective-permute-start(bf16[528,384]{1,0:T(8,128)(2,1)S(1)} %copy-done), channel_id=1, source_target_pairs={{0,128},{1,33},{2,130},{3,35},{4,132},{5,37},{6,134},{7,39},{8,136... | collective-permute-start | bytes 1216520 | tf_op jit(solution)/shard_map/ppermute | solution.py:226
  17.1 7.8 %collective-permute-done.1.s1 = bf16[528,384]{1,0:T(8,128)(2,1)S(1)} collective-permute-done((bf16[528,384]{1,0:T(8,128)(2,1)}, bf16[528,384]{1,0:T(8,128)(2,1)S(1)}, u32[]{:S(2)}, u32[]{:S(2)}) %collective-permute-start.1) | collective-permute-done | bytes 405536 | tf_op jit(solution)/shard_map/ppermute | solution.py:226
  24.8 1.9 %collective-permute-start.3 = (bf16[528,384]{1,0:T(8,128)(2,1)S(1)}, bf16[528,384]{1,0:T(8,128)(2,1)S(1)}, u32[]{:S(2)}, u32[]{:S(2)}) collective-permute-start(bf16[528,384]{1,0:T(8,128)(2,1)S(1)} %collective-permute-done.1.s1), channel_id=1, source_target_pairs={{0,128},{1,33},{2,130},{3,35},{4,132},{5,37},{6,134},{7,39},{8,136... | collective-permute-start | bytes 1216520 | tf_op jit(solution)/shard_map/ppermute | solution.py:226
  26.8 0.0 copy-done.1
  26.8 0.8 %shard_map.60 = (f32[64,64]{1,0:T(8,128)S(1)}, f32[512,128]{1,0:T(8,128)S(1)}) custom-call(bf16[528,384]{1,0:T(8,128)(2,1)S(1)} %copy-done, bf16[64,256]{1,0:T(8,128)(2,1)S(1)} %copy-done.1), custom_call_target="tpu_custom_call" | custom-call | tf_op jit(solution)/shard_map/pallas_call | solution.py:206
  27.6 1.9 %collective-permute-start.5 = (f32[64,64]{1,0:T(8,128)S(1)}, f32[64,64]{1,0:T(8,128)S(1)}, u32[]{:S(2)}, u32[]{:S(2)}) collective-permute-start(f32[64,64]{1,0:T(8,128)S(1)} %get-tuple-element.38.g0), channel_id=1, source_target_pairs={{0,1},{1,0},{2,3},{3,2},{4,5},{5,4},{6,7},{7,6},{8,9},{9,8},{10,11... | collective-permute-start | bytes 49160 | tf_op jit(solution)/shard_map/ppermute | solution.py:230
  29.5 0.1 pad_add_fusion.ids
  29.6 2.2 %shard_map.61 = (f32[512,128]{1,0:T(8,128)S(1)}, f32[512,128]{1,0:T(8,128)S(1)}, f32[16,1024]{1,0:T(8,128)S(1)}) custom-call(s32[4]{0:T(128)S(1)} %pad_add_fusion.ids, bf16[528,384]{1,0:T(8,128)(2,1)S(1)} %copy-done, bf16[528,384]{1,0:T(8,128)(2,1)S(1)} %collective-permute-done.1.s1, bf16[512,256]{1,0:T(8,128)(2,1)S(1)} %collective-permute-done.t1), custom_call_target="tpu_custom_call" | custom-call | tf_op jit(solution)/shard_map/pallas_call | solution.py:206
  31.8 0.0 collective-permute-done.5.s1
  31.8 0.0 collective-permute-done.2.s2
  31.9 0.0 collective-permute-done.4.t23
  31.9 2.8 %collective-permute-done.3.s3 = bf16[528,384]{1,0:T(8,128)(2,1)S(1)} collective-permute-done((bf16[528,384]{1,0:T(8,128)(2,1)S(1)}, bf16[528,384]{1,0:T(8,128)(2,1)S(1)}, u32[]{:S(2)}, u32[]{:S(2)}) %collective-permute-start.3) | collective-permute-done | bytes 405536 | tf_op jit(solution)/shard_map/ppermute | solution.py:226
  34.6 2.7 %shard_map.62 = (bf16[1024,128]{1,0:T(8,128)(2,1)S(1)}, f32[16,1024]{1,0:T(8,128)S(1)}) custom-call(s32[4]{0:T(128)S(1)} %pad_add_fusion.ids, bf16[528,384]{1,0:T(8,128)(2,1)S(1)} %copy-done, bf16[528,384]{1,0:T(8,128)(2,1)S(1)} %collective-permute-done.1.s1, bf16[528,384]{1,0:T(8,128)(2,1)S(1)} %collective-permute-done.2.s2, ...), custom_call_target="tpu_custom_call" | custom-call | tf_op jit(solution)/shard_map/pallas_call | solution.py:206
  37.3 3.4 %collective-permute-start.6 = (bf16[1024,128]{1,0:T(8,128)(2,1)S(1)}, bf16[1024,128]{1,0:T(8,128)(2,1)S(1)}, u32[]{:S(2)}, u32[]{:S(2)}) collective-permute-start(bf16[1024,128]{1,0:T(8,128)(2,1)S(1)} %get-tuple-element.33), channel_id=1, source_target_pairs={{0,32},{1,129},{2,34},{3,131},{4,36},{5,133},{6,38},{7,135},{8,40}... | collective-permute-start | bytes 786440 | tf_op jit(solution)/shard_map/ppermute | solution.py:226
  40.7 1.9 %collective-permute-start.7 = (f32[64,64]{1,0:T(8,128)S(1)}, f32[64,64]{1,0:T(8,128)S(1)}, u32[]{:S(2)}, u32[]{:S(2)}) collective-permute-start(f32[64,64]{1,0:T(8,128)S(1)} %add.8), channel_id=1, source_target_pairs={{0,2},{1,3},{2,0},{3,1},{4,6},{5,7},{6,4},{7,5},{8,10},{9,11},{10,... | collective-permute-start | bytes 49160 | tf_op jit(solution)/shard_map/ppermute | solution.py:230
  42.7 2.1 %shard_map.63 = (f32[512,128]{1,0:T(8,128)S(1)}, f32[512,128]{1,0:T(8,128)S(1)}) custom-call(bf16[528,384]{1,0:T(8,128)(2,1)S(1)} %copy-done, bf16[528,384]{1,0:T(8,128)(2,1)S(1)} %collective-permute-done.1.s1, bf16[528,384]{1,0:T(8,128)(2,1)S(1)} %collective-permute-done.2.s2, bf16[528,384]{1,0:T(8,128)(2,1)S(1)} %collective-permute-done.3.s3, ...), custom_call_target="tpu_custom_call" | custom-call | tf_op jit(solution)/shard_map/pallas_call | solution.py:206
  44.8 1.8 %collective-permute-done.7.s2 = f32[64,64]{1,0:T(8,128)S(1)} collective-permute-done((f32[64,64]{1,0:T(8,128)S(1)}, f32[64,64]{1,0:T(8,128)S(1)}, u32[]{:S(2)}, u32[]{:S(2)}) %collective-permute-start.7) | collective-permute-done | bytes 16416 | tf_op jit(solution)/shard_map/ppermute | solution.py:230
  46.6 0.0 collective-permute-done.6.received.first
  46.6 1.9 %collective-permute-start.8 = (bf16[512,128]{1,0:T(8,128)(2,1)S(1)}, bf16[512,128]{1,0:T(8,128)(2,1)S(1)}, u32[]{:S(2)}, u32[]{:S(2)}) collective-permute-start(bf16[512,128]{1,0:T(8,128)(2,1)S(1)} %shard_map.64), channel_id=1, source_target_pairs={{0,96},{1,385},{2,98},{3,387},{4,100},{5,389},{6,102},{7,391},{8,1... | collective-permute-start | bytes 393224 | tf_op jit(solution)/shard_map/ppermute | solution.py:226
  48.5 3.4 %shard_map.66 = f32[64,192]{1,0:T(8,128)} custom-call(f32[64,64]{1,0:T(8,128)S(1)} %get-tuple-element.38.g0, f32[64,64]{1,0:T(8,128)S(1)} %collective-permute-done.5.s1, f32[64,64]{1,0:T(8,128)S(1)} %collective-permute-done.7.s2), custom_call_target="tpu_custom_call" | custom-call | tf_op jit(solution)/shard_map/pallas_call | solution.py:206
  52.0 1.5 %collective-permute-done.8.second = bf16[512,128]{1,0:T(8,128)(2,1)S(1)} collective-permute-done((bf16[512,128]{1,0:T(8,128)(2,1)S(1)}, bf16[512,128]{1,0:T(8,128)(2,1)S(1)}, u32[]{:S(2)}, u32[]{:S(2)}) %collective-permute-start.8) | collective-permute-done | bytes 131104 | tf_op jit(solution)/shard_map/ppermute | solution.py:226
  53.5 0.7 %shard_map.65 = bf16[512,128]{1,0:T(8,128)(2,1)} custom-call(f32[512,128]{1,0:T(8,128)S(1)} %get-tuple-element.32.own, bf16[1024,128]{1,0:T(8,128)(2,1)S(1)} %collective-permute-done.6.received.first, bf16[512,128]{1,0:T(8,128)(2,1)S(1)} %collective-permute-done.8.second, f32[512,128]{1,0:T(8,128)S(1)} %get-tuple-element.37.scale), custom_call_target="tpu_custom_call" | custom-call | tf_op jit(solution)/shard_map/pallas_call | solution.py:206
  (3 shorter events, 0.1 us)
Async XLA Ops:
  0.6 12.5 %copy-start.2 = (bf16[512,256]{1,0:T(8,128)(2,1)S(1)}, bf16[512,256]{1,0:T(8,128)(2,1)}, u32[]{:S(2)}) copy-start(bf16[512,256]{1,0:T(8,128)(2,1)} %points.1) | copy-start | bytes 786436
  0.6 12.5 %collective-permute-start = (bf16[512,256]{1,0:T(8,128)(2,1)}, bf16[512,256]{1,0:T(8,128)(2,1)S(1)}, u32[]{:S(2)}, u32[]{:S(2)}) collective-permute-start(bf16[512,256]{1,0:T(8,128)(2,1)} %points.1), channel_id=1, source_target_pairs={{0,32},{1,129},{2,34},{3,131},{4,36},{5,133},{6,38},{7,135},{8,40}... | collective-permute-start | bytes 786440 | tf_op jit(solution)/shard_map/ppermute | solution.py:226
  10.6 4.5 %copy-start = (bf16[528,384]{1,0:T(8,128)(2,1)S(1)}, bf16[528,384]{1,0:T(8,128)(2,1)}, u32[]{:S(2)}) copy-start(bf16[528,384]{1,0:T(8,128)(2,1)} %shard_map.59.send.s0) | copy-start | bytes 1216516
  10.6 14.2 %collective-permute-start.1 = (bf16[528,384]{1,0:T(8,128)(2,1)}, bf16[528,384]{1,0:T(8,128)(2,1)S(1)}, u32[]{:S(2)}, u32[]{:S(2)}) collective-permute-start(bf16[528,384]{1,0:T(8,128)(2,1)} %shard_map.59.send.s0), channel_id=1, source_target_pairs={{0,384},{1,97},{2,386},{3,99},{4,388},{5,101},{6,390},{7,103},{8,3... | collective-permute-start | bytes 1216520 | tf_op jit(solution)/shard_map/ppermute | solution.py:226
  13.2 13.6 %copy-start.1 = (bf16[64,256]{1,0:T(8,128)(2,1)S(1)}, bf16[64,256]{1,0:T(8,128)(2,1)}, u32[]{:S(2)}) copy-start(bf16[64,256]{1,0:T(8,128)(2,1)} %proxies) | copy-start | bytes 98308
  13.2 18.7 %collective-permute-start.4 = (bf16[1024,256]{1,0:T(8,128)(2,1)S(1)}, bf16[1024,256]{1,0:T(8,128)(2,1)S(1)}, u32[]{:S(2)}, u32[]{:S(2)}) collective-permute-start(bf16[1024,256]{1,0:T(8,128)(2,1)S(1)} %pad_maximum_fusion), channel_id=1, source_target_pairs={{0,96},{1,385},{2,98},{3,387},{4,100},{5,389},{6,102},{7,391},{8,1... | collective-permute-start | bytes 1572872 | tf_op jit(solution)/shard_map/ppermute | solution.py:226
  15.1 16.7 %collective-permute-start.2 = (bf16[528,384]{1,0:T(8,128)(2,1)S(1)}, bf16[528,384]{1,0:T(8,128)(2,1)S(1)}, u32[]{:S(2)}, u32[]{:S(2)}) collective-permute-start(bf16[528,384]{1,0:T(8,128)(2,1)S(1)} %copy-done), channel_id=1, source_target_pairs={{0,128},{1,33},{2,130},{3,35},{4,132},{5,37},{6,134},{7,39},{8,136... | collective-permute-start | bytes 1216520 | tf_op jit(solution)/shard_map/ppermute | solution.py:226
  24.8 9.8 %collective-permute-start.3 = (bf16[528,384]{1,0:T(8,128)(2,1)S(1)}, bf16[528,384]{1,0:T(8,128)(2,1)S(1)}, u32[]{:S(2)}, u32[]{:S(2)}) collective-permute-start(bf16[528,384]{1,0:T(8,128)(2,1)S(1)} %collective-permute-done.1.s1), channel_id=1, source_target_pairs={{0,128},{1,33},{2,130},{3,35},{4,132},{5,37},{6,134},{7,39},{8,136... | collective-permute-start | bytes 1216520 | tf_op jit(solution)/shard_map/ppermute | solution.py:226
  27.6 4.2 %collective-permute-start.5 = (f32[64,64]{1,0:T(8,128)S(1)}, f32[64,64]{1,0:T(8,128)S(1)}, u32[]{:S(2)}, u32[]{:S(2)}) collective-permute-start(f32[64,64]{1,0:T(8,128)S(1)} %get-tuple-element.38.g0), channel_id=1, source_target_pairs={{0,1},{1,0},{2,3},{3,2},{4,5},{5,4},{6,7},{7,6},{8,9},{9,8},{10,11... | collective-permute-start | bytes 49160 | tf_op jit(solution)/shard_map/ppermute | solution.py:230
  37.3 9.2 %collective-permute-start.6 = (bf16[1024,128]{1,0:T(8,128)(2,1)S(1)}, bf16[1024,128]{1,0:T(8,128)(2,1)S(1)}, u32[]{:S(2)}, u32[]{:S(2)}) collective-permute-start(bf16[1024,128]{1,0:T(8,128)(2,1)S(1)} %get-tuple-element.33), channel_id=1, source_target_pairs={{0,32},{1,129},{2,34},{3,131},{4,36},{5,133},{6,38},{7,135},{8,40}... | collective-permute-start | bytes 786440 | tf_op jit(solution)/shard_map/ppermute | solution.py:226
  40.7 5.8 %collective-permute-start.7 = (f32[64,64]{1,0:T(8,128)S(1)}, f32[64,64]{1,0:T(8,128)S(1)}, u32[]{:S(2)}, u32[]{:S(2)}) collective-permute-start(f32[64,64]{1,0:T(8,128)S(1)} %add.8), channel_id=1, source_target_pairs={{0,2},{1,3},{2,0},{3,1},{4,6},{5,7},{6,4},{7,5},{8,10},{9,11},{10,... | collective-permute-start | bytes 49160 | tf_op jit(solution)/shard_map/ppermute | solution.py:230
  46.6 6.9 %collective-permute-start.8 = (bf16[512,128]{1,0:T(8,128)(2,1)S(1)}, bf16[512,128]{1,0:T(8,128)(2,1)S(1)}, u32[]{:S(2)}, u32[]{:S(2)}) collective-permute-start(bf16[512,128]{1,0:T(8,128)(2,1)S(1)} %shard_map.64), channel_id=1, source_target_pairs={{0,96},{1,385},{2,98},{3,387},{4,100},{5,389},{6,102},{7,391},{8,1... | collective-permute-start | bytes 393224 | tf_op jit(solution)/shard_map/ppermute | solution.py:226

commit v3 on v2

--- a/solution.py
+++ b/solution.py
@@ -20,6 +20,7 @@
 GROUP = 64
 LOG2E = 1.4426950408889634
 LINE = 4
+MASKS = (0, 1, 3, 2)
 PANEL = 4
 NT = (((1,), (1,)), ((), ()))
 HIGH = lax.Precision.HIGHEST
@@ -42,35 +43,46 @@
     return dot_nt(ones, hi) + dot_nt(ones, lo)
 
 
-def send_kernel(points, weights, near, send, ids, sems):
-    copies = [
-        pltpu.make_async_copy(points, send.at[pl.ds(0, UNIT), pl.ds(0, DIM)], sems.at[0]),
+def send_kernel(points, weights, near, send, held, ids, sems):
+    unit, left, right = pl.ds(0, UNIT), pl.ds(0, DIM), pl.ds(DIM, NV)
+    arriving = [
+        pltpu.make_async_copy(points, held.at[unit, left], sems.at[0]),
         pltpu.make_async_copy(near, ids, sems.at[1]),
-        pltpu.make_async_copy(weights, send.at[pl.ds(0, UNIT), pl.ds(DIM, NV)], sems.at[2]),
+        pltpu.make_async_copy(weights, held.at[unit, right], sems.at[2]),
     ]
-    for copy in copies:
+    leaving = [
+        pltpu.make_async_copy(held.at[unit, left], send.at[unit, left], sems.at[3]),
+        pltpu.make_async_copy(held.at[unit, right], send.at[unit, right], sems.at[4]),
+        pltpu.make_async_copy(held.at[pl.ds(UNIT, EXTRA), :], send.at[pl.ds(UNIT, EXTRA), :], sems.at[5]),
+    ]
+    for copy in arriving:
         copy.start()
-    send[UNIT:, BLK:] = jnp.zeros((EXTRA, DIM + NV - BLK), jnp.bfloat16)
-    copies[1].wait()
+    held[UNIT:, BLK:] = jnp.zeros((EXTRA, DIM + NV - BLK), jnp.bfloat16)
+    arriving[1].wait()
     local = ids[...] & (GROUP - 1)
     lanes = lax.broadcasted_iota(jnp.int32, (NB, BLK), 1)
     counts = jnp.zeros((NB, BLK), jnp.float32)
     for t in range(near.shape[1]):
         counts = counts + jnp.where(local[:, t : t + 1] == lanes, 1.0, 0.0)
-    copies[0].wait()
-    f = send[:UNIT, :DIM].astype(jnp.float32)
+    arriving[0].wait()
+    leaving[0].start()
+    arriving[2].wait()
+    leaving[1].start()
+    f = held[:UNIT, :DIM].astype(jnp.float32)
     norm = row_norms(split2(f * f))
     rows = jnp.concatenate([norm[0:1, b * BLK : (b + 1) * BLK] for b in range(NB)], axis=0)
     first = rows.astype(jnp.bfloat16).astype(jnp.float32)
     second = (rows - first).astype(jnp.bfloat16).astype(jnp.float32)
     third = rows - first - second
     extra = jnp.concatenate([counts, first, second, third], axis=0)
-    send[UNIT:, :BLK] = extra.astype(jnp.bfloat16)
-    copies[2].wait()
-
-
-def gram_kernel(send, proxies, gram, scale):
-    p = send[:UNIT, :DIM]
+    held[UNIT:, :BLK] = extra.astype(jnp.bfloat16)
+    leaving[2].start()
+    for copy in leaving:
+        copy.wait()
+
+
+def gram_kernel(points, proxies, gram, scale):
+    p = points[...]
     f = p.astype(jnp.float32)
     squares = split2(f * f)
     tall = jnp.ones((DIM, NV), jnp.bfloat16)
@@ -139,12 +151,14 @@
     out[:, 2 * RANK :] = uppers[2]
 
 
-def bias_rows(ids, sources, bias):
+def bias_rows(sources, bias):
+    row, odd = lax.axis_index("row"), lax.axis_index("col") & 1
     rows = lax.broadcasted_iota(jnp.int32, (LINE * NB, BLK), 0)
     lanes = lax.broadcasted_iota(jnp.int32, (LINE * NB, BLK), 1)
     wanted = jnp.zeros((LINE * NB, BLK), jnp.int32)
-    for k in range(LINE):
-        wanted = jnp.where(rows // NB == k, ids[k] * NB + rows % NB, wanted)
+    for k, mask in enumerate(MASKS):
+        unit = row ^ (mask * (1 + (SIDE - 1) * odd))
+        wanted = jnp.where(rows // NB == k, unit * NB + rows % NB, wanted)
     pick = jnp.where(wanted == lanes, 1.0, 0.0).astype(jnp.bfloat16)
     for k, source in enumerate(sources):
         extra = source[UNIT:ROWS, :BLK]
@@ -174,22 +188,23 @@
     return total
 
 
-def near_first_kernel(ids, s0, s1, t1, own, other, bias):
-    bias_rows(ids, (s0, s1), bias)
+def near_first_kernel(s0, s1, t1, t23, own, *rest):
+    others, bias = rest[:-1], rest[-1]
+    bias_rows((s0, s1), bias)
     own[...] = near_sum(s0[:UNIT, :DIM], 0, (s0, s1), bias)
-    other[...] = near_sum(t1[...], 1, (s0, s1), bias)
-
-
-def near_out_kernel(ids, s0, s1, s2, s3, t1, t23, other, bias01, out, bias):
-    bias_rows(ids, (s2, s3), bias)
-    total = near_sum(t23[UNIT:, :], 3, (s0, s1), bias01)
-    out[UNIT:, :] = near_sum(t23[UNIT:, :], 3, (s2, s3), bias, total).astype(jnp.bfloat16)
-    out[:UNIT, :] = near_sum(t1[...], 1, (s2, s3), bias, other[...]).astype(jnp.bfloat16)
-
-
-def near_in_kernel(s0, s1, s2, s3, t23, own, bias01, bias, own_out, out):
-    total = near_sum(t23[:UNIT, :], 2, (s0, s1), bias01)
-    out[...] = near_sum(t23[:UNIT, :], 2, (s2, s3), bias, total)
+    lefts = (t1, t23.at[pl.ds(0, UNIT)], t23.at[pl.ds(UNIT, UNIT)])
+    for t, (left, other) in enumerate(zip(lefts, others), 1):
+        other[...] = near_sum(left[...], t, (s0, s1), bias)
+
+
+def near_out_kernel(s2, s3, t1, t23, total1, total3, out, bias):
+    bias_rows((s2, s3), bias)
+    out[UNIT:, :] = near_sum(t23[UNIT:, :], 3, (s2, s3), bias, total3[...]).astype(jnp.bfloat16)
+    out[:UNIT, :] = near_sum(t1[...], 1, (s2, s3), bias, total1[...]).astype(jnp.bfloat16)
+
+
+def near_in_kernel(s0, s2, s3, t23, own, total2, bias, own_out, out):
+    out[...] = near_sum(t23[:UNIT, :], 2, (s2, s3), bias, total2[...])
     own_out[...] = near_sum(s0[:UNIT, :DIM], 0, (s2, s3), bias, own[...])
 
 
@@ -202,15 +217,15 @@
     out[...] = (total * scale[...]).astype(jnp.bfloat16)
 
 
-def call(kernel, shapes, *args, scratch=(), scalars=0, space=pltpu.VMEM, vmem=VMEM):
+def call(kernel, shapes, *args, micros=1.0, scratch=(), space=pltpu.VMEM, vmem=VMEM):
     return pl.pallas_call(
         kernel,
         out_shape=shapes,
-        in_specs=[pl.BlockSpec(memory_space=pltpu.SMEM)] * scalars
-        + [pl.BlockSpec(memory_space=space)] * (len(args) - scalars),
-        out_specs=jax.tree.map(lambda _: pl.BlockSpec(memory_space=pltpu.VMEM), shapes),
+        in_specs=[pl.BlockSpec(memory_space=space)] * len(args),
+        out_specs=jax.tree.map(lambda _: pl.BlockSpec(memory_space=space), shapes),
         scratch_shapes=list(scratch),
         compiler_params=pltpu.CompilerParams(vmem_limit_bytes=vmem),
+        cost_estimate=pl.CostEstimate(flops=int(micros * 1e9), bytes_accessed=int(micros * 3e6), transcendentals=0),
     )(*args)
 
 
@@ -240,7 +255,11 @@
         points,
         weights,
         near_blocks,
-        scratch=[pltpu.VMEM(near_blocks.shape, jnp.int32), pltpu.SemaphoreType.DMA((3,))],
+        scratch=[
+            pltpu.VMEM((ROWS, DIM + NV), bf16),
+            pltpu.VMEM(near_blocks.shape, jnp.int32),
+            pltpu.SemaphoreType.DMA((6,)),
+        ],
         space=pltpu.HBM,
         vmem=SEND_VMEM,
     )
@@ -248,39 +267,32 @@
     s2 = exchange(send, 1, 1)
     t23 = exchange(jnp.concatenate([points, t1], axis=0), 3, 0)
     proxies, t1 = lax.optimization_barrier((proxies, t1))
-    gram, scale = call(gram_kernel, (shape((RANK, RANK), f32), shape((UNIT, NV), f32)), send, proxies)
+    gram, scale = call(gram_kernel, (shape((RANK, RANK), f32), shape((UNIT, NV), f32)), points, proxies)
     s3 = exchange(s1, 1, 1)
     gram, s1 = lax.optimization_barrier((gram, s1))
     g1 = partner(gram, 1)
-    row = lax.axis_index("row")
-    odd = lax.axis_index("col") % 2
-    ids = jnp.stack([jnp.where(odd == 1, row ^ (m * SIDE), row ^ m) for m in (0, 1, 3, 2)]).astype(jnp.int32)
     half = shape((LINE * NB, 2 * UNIT), f32)
     unit = shape((UNIT, NV), f32)
-    own, other, bias01 = call(near_first_kernel, (unit, unit, half), ids, send, s1, t1, scalars=1)
-    level1, later_ids = lax.optimization_barrier((gram + g1, ids))
-    g2 = partner(level1, 2)
-    out, bias23 = call(
-        near_out_kernel,
-        (shape((2 * UNIT, NV), bf16), half),
-        later_ids,
+    own, total1, total2, total3 = call(
+        near_first_kernel,
+        (unit,) * LINE,
         send,
         s1,
-        s2,
-        s3,
         t1,
         t23,
-        other,
-        bias01,
-        scalars=1,
+        scratch=[pltpu.VMEM(half.shape, f32)],
+    )
+    g1, total1 = lax.optimization_barrier((g1, total1))
+    g2 = partner(gram + g1, 2)
+    out, bias23 = call(
+        near_out_kernel, (shape((2 * UNIT, NV), bf16), half), s2, s3, t1, t23, total1, total3
     )
     r1 = exchange(out, 1, 0)
-    own, mine = call(near_in_kernel, (unit, unit), send, s1, s2, s3, t23, own, bias01, bias23)
-    mine, g2 = lax.optimization_barrier((mine, g2))
+    own, mine = call(near_in_kernel, (unit, unit), send, s2, s3, t23, own, total2, bias23)
     relayed = call(relay_kernel, shape((UNIT, NV), bf16), mine, r1)
     r2 = exchange(relayed, 3, 0)
     gram, own = lax.optimization_barrier((gram, own))
-    factors = call(factor_kernel, shape((RANK, 3 * RANK), f32), gram, g1, g2)
+    factors = call(factor_kernel, shape((RANK, 3 * RANK), f32), gram, g1, g2, micros=3.4)
     near_product = call(finish_kernel, shape((UNIT, NV), bf16), own, r1, r2, scale)
     return (near_product, factors)
 

time: 54.6 us -> 52.9 us (0.969)
  the two profiles are of different devices: /device:TPU:2 before, /device:TPU:8 now
where the time goes in v3:
time: 52.9 us; the launch traced here: 52.5 us
  starting transfers between devices  33.6 us (64%)
  Pallas kernels  12.6 us (24%)
  waiting for transfers between devices  5.49 us (10%)
  between operations  0.84 us (2%)
    ppermute x7, starting transfers between devices, exchange(): return lax.ppermute(value, ('row', 'col'), pairs)  29.7 us
    pallas_call x8, Pallas kernels, call(): pl.pallas_call(kernel, out_shape=shapes, in_specs=[pl.BlockSpec(memory_sp...  12.6 us
    ppermute x7, waiting for transfers between devices, exchange(): return lax.ppermute(value, ('row', 'col'), pairs)  5.49 us
    ppermute x2, starting transfers between devices, partner(): lax.ppermute(value, 'col', [(c, c ^ mask) for c in range(lax.axis_size('c...  3.85 us
  transfers between devices with their start and end apart: 9, of which 3 were waited for; matrix products, arithmetic and copies ran while one was open for 0% of the time, Pallas kernels for 20%

profile of v3, /device:TPU:8, one launch (start us, length us, event | category | flops | bytes accessed | tf_op | source)
XLA Modules:
  0.0 52.5 jit_solution(10899742823991039766)
XLA Ops:
  0.6 0.0 copy-start
  0.6 3.5 %collective-permute-start = (bf16[512,256]{1,0:T(8,128)(2,1)}, bf16[512,256]{1,0:T(8,128)(2,1)S(1)}, u32[]{:S(2)}, u32[]{:S(2)}) collective-permute-start(bf16[512,256]{1,0:T(8,128)(2,1)} %points.3), channel_id=1, source_target_pairs={{0,32},{1,129},{2,34},{3,131},{4,36},{5,133},{6,38},{7,135},{8,40}... | collective-permute-start | bytes 786440 | tf_op jit(solution)/shard_map/ppermute | solution.py:241
  4.2 1.9 %shard_map.60.s0 = bf16[528,384]{1,0:T(8,128)(2,1)} custom-call(bf16[512,256]{1,0:T(8,128)(2,1)} %points.3, bf16[512,128]{1,0:T(8,128)(2,1)} %weights.1, s32[4,16]{1,0:T(4,128)} %near.1), custom_call_target="tpu_custom_call" | custom-call | flops 1000000000 | bytes 3000000 | tf_op jit(solution)/shard_map/pallas_call | solution.py:221
  6.1 0.0 copy-start.1
  6.1 0.0 copy-start.2
  6.1 3.6 %collective-permute-start.1 = (bf16[528,384]{1,0:T(8,128)(2,1)}, bf16[528,384]{1,0:T(8,128)(2,1)S(1)}, u32[]{:S(2)}, u32[]{:S(2)}) collective-permute-start(bf16[528,384]{1,0:T(8,128)(2,1)} %shard_map.60.s0), channel_id=1, source_target_pairs={{0,384},{1,97},{2,386},{3,99},{4,388},{5,101},{6,390},{7,103},{8,3... | collective-permute-start | bytes 1216520 | tf_op jit(solution)/shard_map/ppermute | solution.py:241
  9.8 0.0 collective-permute-done.t1
  9.8 0.0 copy-done
  9.8 4.1 %collective-permute-start.4 = (bf16[1024,256]{1,0:T(8,128)(2,1)S(1)}, bf16[1024,256]{1,0:T(8,128)(2,1)S(1)}, u32[]{:S(2)}, u32[]{:S(2)}) collective-permute-start(bf16[1024,256]{1,0:T(8,128)(2,1)S(1)} %pad_maximum_fusion), channel_id=1, source_target_pairs={{0,96},{1,385},{2,98},{3,387},{4,100},{5,389},{6,102},{7,391},{8,1... | collective-permute-start | bytes 1572872 | tf_op jit(solution)/shard_map/ppermute | solution.py:241
  14.0 0.0 copy-done.1
  14.0 5.0 %collective-permute-start.2 = (bf16[528,384]{1,0:T(8,128)(2,1)S(1)}, bf16[528,384]{1,0:T(8,128)(2,1)S(1)}, u32[]{:S(2)}, u32[]{:S(2)}) collective-permute-start(bf16[528,384]{1,0:T(8,128)(2,1)S(1)} %copy-done.1), channel_id=1, source_target_pairs={{0,128},{1,33},{2,130},{3,35},{4,132},{5,37},{6,134},{7,39},{8,136... | collective-permute-start | bytes 1216520 | tf_op jit(solution)/shard_map/ppermute | solution.py:241
  19.0 0.0 collective-permute-done.1.s1
  19.0 9.1 %collective-permute-start.3 = (bf16[528,384]{1,0:T(8,128)(2,1)S(1)}, bf16[528,384]{1,0:T(8,128)(2,1)S(1)}, u32[]{:S(2)}, u32[]{:S(2)}) collective-permute-start(bf16[528,384]{1,0:T(8,128)(2,1)S(1)} %collective-permute-done.1.s1), channel_id=1, source_target_pairs={{0,128},{1,33},{2,130},{3,35},{4,132},{5,37},{6,134},{7,39},{8,136... | collective-permute-start | bytes 1216520 | tf_op jit(solution)/shard_map/ppermute | solution.py:241
  28.1 0.0 copy-done.2
  28.1 0.8 %shard_map.59 = (f32[64,64]{1,0:T(8,128)S(1)}, f32[512,128]{1,0:T(8,128)S(1)}) custom-call(bf16[512,256]{1,0:T(8,128)(2,1)S(1)} %copy-done, bf16[64,256]{1,0:T(8,128)(2,1)S(1)} %copy-done.2), custom_call_target="tpu_custom_call" | custom-call | flops 1000000000 | bytes 3000000 | tf_op jit(solution)/shard_map/pallas_call | solution.py:221
  28.9 1.9 %collective-permute-start.5 = (f32[64,64]{1,0:T(8,128)S(1)}, f32[64,64]{1,0:T(8,128)S(1)}, u32[]{:S(2)}, u32[]{:S(2)}) collective-permute-start(f32[64,64]{1,0:T(8,128)S(1)} %get-tuple-element.36.g0), channel_id=1, source_target_pairs={{0,1},{1,0},{2,3},{3,2},{4,5},{5,4},{6,7},{7,6},{8,9},{9,8},{10,11... | collective-permute-start | bytes 49160 | tf_op jit(solution)/shard_map/ppermute | solution.py:245
  30.8 0.0 collective-permute-done.4.t23
  30.8 2.8 %shard_map.61 = (f32[512,128]{1,0:T(8,128)S(1)}, f32[512,128]{1,0:T(8,128)S(1)}, f32[512,128]{1,0:T(8,128)S(1)}, f32[512,128]{1,0:T(8,128)S(1)}) custom-call(bf16[528,384]{1,0:T(8,128)(2,1)S(1)} %copy-done.1, bf16[528,384]{1,0:T(8,128)(2,1)S(1)} %collective-permute-done.1.s1, bf16[512,256]{1,0:T(8,128)(2,1)S(1)} %collective-permute-done.t1, ...), custom_call_target="tpu_custom_call" | custom-call | flops 1000000000 | bytes 3000000 | tf_op jit(solution)/shard_map/pallas_call | solution.py:221
  33.6 0.0 collective-permute-done.5.s1
  33.6 0.0 collective-permute-done.2.s2
  33.6 0.3 collective-permute-done.3.s3
  33.9 1.5 %shard_map.62 = (bf16[1024,128]{1,0:T(8,128)(2,1)S(1)}, f32[16,1024]{1,0:T(8,128)S(1)}) custom-call(bf16[528,384]{1,0:T(8,128)(2,1)S(1)} %collective-permute-done.2.s2, bf16[528,384]{1,0:T(8,128)(2,1)S(1)} %collective-permute-done.3.s3, bf16[512,256]{1,0:T(8,128)(2,1)S(1)} %collective-permute-done.t1, bf16[1024,256]{1,0:T(8,128)(2,1)S(1)} %collective-permute-done.4.t23, ...), custom_call_target="tpu_custom_call" | custom-call | flops 1000000000 | bytes 3000000 | tf_op jit(solution)/shard_map/pallas_call | solution.py:221
  35.4 2.4 %collective-permute-start.6 = (bf16[1024,128]{1,0:T(8,128)(2,1)S(1)}, bf16[1024,128]{1,0:T(8,128)(2,1)S(1)}, u32[]{:S(2)}, u32[]{:S(2)}) collective-permute-start(bf16[1024,128]{1,0:T(8,128)(2,1)S(1)} %get-tuple-element.33), channel_id=1, source_target_pairs={{0,32},{1,129},{2,34},{3,131},{4,36},{5,133},{6,38},{7,135},{8,40}... | collective-permute-start | bytes 786440 | tf_op jit(solution)/shard_map/ppermute | solution.py:241
  37.9 1.9 %collective-permute-start.8 = (f32[64,64]{1,0:T(8,128)S(1)}, f32[64,64]{1,0:T(8,128)S(1)}, u32[]{:S(2)}, u32[]{:S(2)}) collective-permute-start(f32[64,64]{1,0:T(8,128)S(1)} %add.3), channel_id=1, source_target_pairs={{0,2},{1,3},{2,0},{3,1},{4,6},{5,7},{6,4},{7,5},{8,10},{9,11},{10,... | collective-permute-start | bytes 49160 | tf_op jit(solution)/shard_map/ppermute | solution.py:245
  39.8 1.4 %shard_map.63 = (f32[512,128]{1,0:T(8,128)S(1)}, f32[512,128]{1,0:T(8,128)S(1)}) custom-call(bf16[528,384]{1,0:T(8,128)(2,1)S(1)} %copy-done.1, bf16[528,384]{1,0:T(8,128)(2,1)S(1)} %collective-permute-done.2.s2, bf16[528,384]{1,0:T(8,128)(2,1)S(1)} %collective-permute-done.3.s3, bf16[1024,256]{1,0:T(8,128)(2,1)S(1)} %collective-permute-done.4.t23, ...), custom_call_target="tpu_custom_call" | custom-call | flops 1000000000 | bytes 3000000 | tf_op jit(solution)/shard_map/pallas_call | solution.py:221
  41.2 2.5 %collective-permute-done.6.received.first = bf16[1024,128]{1,0:T(8,128)(2,1)S(1)} collective-permute-done((bf16[1024,128]{1,0:T(8,128)(2,1)S(1)}, bf16[1024,128]{1,0:T(8,128)(2,1)S(1)}, u32[]{:S(2)}, u32[]{:S(2)}) %collective-permute-start.6) | collective-permute-done | bytes 262176 | tf_op jit(solution)/shard_map/ppermute | solution.py:241
  43.7 1.9 %collective-permute-start.7 = (bf16[512,128]{1,0:T(8,128)(2,1)S(1)}, bf16[512,128]{1,0:T(8,128)(2,1)S(1)}, u32[]{:S(2)}, u32[]{:S(2)}) collective-permute-start(bf16[512,128]{1,0:T(8,128)(2,1)S(1)} %shard_map.64), channel_id=1, source_target_pairs={{0,96},{1,385},{2,98},{3,387},{4,100},{5,389},{6,102},{7,391},{8,1... | collective-permute-start | bytes 393224 | tf_op jit(solution)/shard_map/ppermute | solution.py:241
  45.6 0.0 collective-permute-done.8.s2
  45.7 3.4 %shard_map.66 = f32[64,192]{1,0:T(8,128)} custom-call(f32[64,64]{1,0:T(8,128)S(1)} %get-tuple-element.36.g0, f32[64,64]{1,0:T(8,128)S(1)} %collective-permute-done.5.s1, f32[64,64]{1,0:T(8,128)S(1)} %collective-permute-done.8.s2), custom_call_target="tpu_custom_call" | custom-call | flops 3400000000 | bytes 10200000 | tf_op jit(solution)/shard_map/pallas_call | solution.py:221
  49.1 2.7 %collective-permute-done.7.second = bf16[512,128]{1,0:T(8,128)(2,1)S(1)} collective-permute-done((bf16[512,128]{1,0:T(8,128)(2,1)S(1)}, bf16[512,128]{1,0:T(8,128)(2,1)S(1)}, u32[]{:S(2)}, u32[]{:S(2)}) %collective-permute-start.7) | collective-permute-done | bytes 131104 | tf_op jit(solution)/shard_map/ppermute | solution.py:241
  51.8 0.7 %shard_map.65 = bf16[512,128]{1,0:T(8,128)(2,1)} custom-call(f32[512,128]{1,0:T(8,128)S(1)} %get-tuple-element.32.own, bf16[1024,128]{1,0:T(8,128)(2,1)S(1)} %collective-permute-done.6.received.first, bf16[512,128]{1,0:T(8,128)(2,1)S(1)} %collective-permute-done.7.second, f32[512,128]{1,0:T(8,128)S(1)} %get-tuple-element.35.scale), custom_call_target="tpu_custom_call" | custom-call | flops 1000000000 | bytes 3000000 | tf_op jit(solution)/shard_map/pallas_call | solution.py:221
  (3 shorter events, 0.1 us)
Async XLA Ops:
  0.6 9.1 %copy-start = (bf16[512,256]{1,0:T(8,128)(2,1)S(1)}, bf16[512,256]{1,0:T(8,128)(2,1)}, u32[]{:S(2)}) copy-start(bf16[512,256]{1,0:T(8,128)(2,1)} %points.3) | copy-start | bytes 786436
  0.6 9.1 %collective-permute-start = (bf16[512,256]{1,0:T(8,128)(2,1)}, bf16[512,256]{1,0:T(8,128)(2,1)S(1)}, u32[]{:S(2)}, u32[]{:S(2)}) collective-permute-start(bf16[512,256]{1,0:T(8,128)(2,1)} %points.3), channel_id=1, source_target_pairs={{0,32},{1,129},{2,34},{3,131},{4,36},{5,133},{6,38},{7,135},{8,40}... | collective-permute-start | bytes 786440 | tf_op jit(solution)/shard_map/ppermute | solution.py:241
  6.1 7.9 %copy-start.1 = (bf16[528,384]{1,0:T(8,128)(2,1)S(1)}, bf16[528,384]{1,0:T(8,128)(2,1)}, u32[]{:S(2)}) copy-start(bf16[528,384]{1,0:T(8,128)(2,1)} %shard_map.60.s0) | copy-start | bytes 1216516
  6.1 22.0 %copy-start.2 = (bf16[64,256]{1,0:T(8,128)(2,1)S(1)}, bf16[64,256]{1,0:T(8,128)(2,1)}, u32[]{:S(2)}) copy-start(bf16[64,256]{1,0:T(8,128)(2,1)} %proxies) | copy-start | bytes 98308
  6.1 12.8 %collective-permute-start.1 = (bf16[528,384]{1,0:T(8,128)(2,1)}, bf16[528,384]{1,0:T(8,128)(2,1)S(1)}, u32[]{:S(2)}, u32[]{:S(2)}) collective-permute-start(bf16[528,384]{1,0:T(8,128)(2,1)} %shard_map.60.s0), channel_id=1, source_target_pairs={{0,384},{1,97},{2,386},{3,99},{4,388},{5,101},{6,390},{7,103},{8,3... | collective-permute-start | bytes 1216520 | tf_op jit(solution)/shard_map/ppermute | solution.py:241
  9.8 21.0 %collective-permute-start.4 = (bf16[1024,256]{1,0:T(8,128)(2,1)S(1)}, bf16[1024,256]{1,0:T(8,128)(2,1)S(1)}, u32[]{:S(2)}, u32[]{:S(2)}) collective-permute-start(bf16[1024,256]{1,0:T(8,128)(2,1)S(1)} %pad_maximum_fusion), channel_id=1, source_target_pairs={{0,96},{1,385},{2,98},{3,387},{4,100},{5,389},{6,102},{7,391},{8,1... | collective-permute-start | bytes 1572872 | tf_op jit(solution)/shard_map/ppermute | solution.py:241
  14.0 19.6 %collective-permute-start.2 = (bf16[528,384]{1,0:T(8,128)(2,1)S(1)}, bf16[528,384]{1,0:T(8,128)(2,1)S(1)}, u32[]{:S(2)}, u32[]{:S(2)}) collective-permute-start(bf16[528,384]{1,0:T(8,128)(2,1)S(1)} %copy-done.1), channel_id=1, source_target_pairs={{0,128},{1,33},{2,130},{3,35},{4,132},{5,37},{6,134},{7,39},{8,136... | collective-permute-start | bytes 1216520 | tf_op jit(solution)/shard_map/ppermute | solution.py:241
  19.0 15.0 %collective-permute-start.3 = (bf16[528,384]{1,0:T(8,128)(2,1)S(1)}, bf16[528,384]{1,0:T(8,128)(2,1)S(1)}, u32[]{:S(2)}, u32[]{:S(2)}) collective-permute-start(bf16[528,384]{1,0:T(8,128)(2,1)S(1)} %collective-permute-done.1.s1), channel_id=1, source_target_pairs={{0,128},{1,33},{2,130},{3,35},{4,132},{5,37},{6,134},{7,39},{8,136... | collective-permute-start | bytes 1216520 | tf_op jit(solution)/shard_map/ppermute | solution.py:241
  28.9 4.7 %collective-permute-start.5 = (f32[64,64]{1,0:T(8,128)S(1)}, f32[64,64]{1,0:T(8,128)S(1)}, u32[]{:S(2)}, u32[]{:S(2)}) collective-permute-start(f32[64,64]{1,0:T(8,128)S(1)} %get-tuple-element.36.g0), channel_id=1, source_target_pairs={{0,1},{1,0},{2,3},{3,2},{4,5},{5,4},{6,7},{7,6},{8,9},{9,8},{10,11... | collective-permute-start | bytes 49160 | tf_op jit(solution)/shard_map/ppermute | solution.py:245
  35.4 8.3 %collective-permute-start.6 = (bf16[1024,128]{1,0:T(8,128)(2,1)S(1)}, bf16[1024,128]{1,0:T(8,128)(2,1)S(1)}, u32[]{:S(2)}, u32[]{:S(2)}) collective-permute-start(bf16[1024,128]{1,0:T(8,128)(2,1)S(1)} %get-tuple-element.33), channel_id=1, source_target_pairs={{0,32},{1,129},{2,34},{3,131},{4,36},{5,133},{6,38},{7,135},{8,40}... | collective-permute-start | bytes 786440 | tf_op jit(solution)/shard_map/ppermute | solution.py:241
  37.9 7.8 %collective-permute-start.8 = (f32[64,64]{1,0:T(8,128)S(1)}, f32[64,64]{1,0:T(8,128)S(1)}, u32[]{:S(2)}, u32[]{:S(2)}) collective-permute-start(f32[64,64]{1,0:T(8,128)S(1)} %add.3), channel_id=1, source_target_pairs={{0,2},{1,3},{2,0},{3,1},{4,6},{5,7},{6,4},{7,5},{8,10},{9,11},{10,... | collective-permute-start | bytes 49160 | tf_op jit(solution)/shard_map/ppermute | solution.py:245
  43.7 8.1 %collective-permute-start.7 = (bf16[512,128]{1,0:T(8,128)(2,1)S(1)}, bf16[512,128]{1,0:T(8,128)(2,1)S(1)}, u32[]{:S(2)}, u32[]{:S(2)}) collective-permute-start(bf16[512,128]{1,0:T(8,128)(2,1)S(1)} %shard_map.64), channel_id=1, source_target_pairs={{0,96},{1,385},{2,98},{3,387},{4,100},{5,389},{6,102},{7,391},{8,1... | collective-permute-start | bytes 393224 | tf_op jit(solution)/shard_map/ppermute | solution.py:241

commit v4 on v3

--- a/solution.py
+++ b/solution.py
@@ -188,24 +188,24 @@
     return total
 
 
-def near_first_kernel(s0, s1, t1, t23, own, *rest):
-    others, bias = rest[:-1], rest[-1]
-    bias_rows((s0, s1), bias)
-    own[...] = near_sum(s0[:UNIT, :DIM], 0, (s0, s1), bias)
-    lefts = (t1, t23.at[pl.ds(0, UNIT)], t23.at[pl.ds(UNIT, UNIT)])
-    for t, (left, other) in enumerate(zip(lefts, others), 1):
-        other[...] = near_sum(left[...], t, (s0, s1), bias)
-
-
-def near_out_kernel(s2, s3, t1, t23, total1, total3, out, bias):
-    bias_rows((s2, s3), bias)
-    out[UNIT:, :] = near_sum(t23[UNIT:, :], 3, (s2, s3), bias, total3[...]).astype(jnp.bfloat16)
-    out[:UNIT, :] = near_sum(t1[...], 1, (s2, s3), bias, total1[...]).astype(jnp.bfloat16)
-
-
-def near_in_kernel(s0, s2, s3, t23, own, total2, bias, own_out, out):
-    out[...] = near_sum(t23[:UNIT, :], 2, (s2, s3), bias, total2[...])
-    own_out[...] = near_sum(s0[:UNIT, :DIM], 0, (s2, s3), bias, own[...])
+def near_first_kernel(s0, s1, s2, t1, own, total1, bias):
+    sources = (s0, s1, s2)
+    bias_rows(sources, bias)
+    own[...] = near_sum(s0[:UNIT, :DIM], 0, sources, bias)
+    total1[...] = near_sum(t1[...], 1, sources, bias)
+
+
+def near_out_kernel(s0, s1, s2, s3, t1, t23, total1, bias, out, last):
+    bias_rows((s3,), last)
+    total3 = near_sum(t23[UNIT:, :], 3, (s0, s1, s2), bias)
+    out[UNIT:, :] = near_sum(t23[UNIT:, :], 3, (s3,), last, total3).astype(jnp.bfloat16)
+    out[:UNIT, :] = near_sum(t1[...], 1, (s3,), last, total1[...]).astype(jnp.bfloat16)
+
+
+def near_in_kernel(s0, s1, s2, s3, t23, own, bias, last, own_out, out):
+    total2 = near_sum(t23[:UNIT, :], 2, (s0, s1, s2), bias)
+    out[...] = near_sum(t23[:UNIT, :], 2, (s3,), last, total2)
+    own_out[...] = near_sum(s0[:UNIT, :DIM], 0, (s3,), last, own[...])
 
 
 def relay_kernel(mine, received, out):
@@ -269,26 +269,26 @@
     proxies, t1 = lax.optimization_barrier((proxies, t1))
     gram, scale = call(gram_kernel, (shape((RANK, RANK), f32), shape((UNIT, NV), f32)), points, proxies)
     s3 = exchange(s1, 1, 1)
-    gram, s1 = lax.optimization_barrier((gram, s1))
+    unit = shape((UNIT, NV), f32)
+    own, total1, bias = call(
+        near_first_kernel, (unit, unit, shape((LINE * NB, 3 * UNIT), f32)), send, s1, s2, t1, micros=20.0
+    )
+    gram, total1 = lax.optimization_barrier((gram, total1))
     g1 = partner(gram, 1)
-    half = shape((LINE * NB, 2 * UNIT), f32)
-    unit = shape((UNIT, NV), f32)
-    own, total1, total2, total3 = call(
-        near_first_kernel,
-        (unit,) * LINE,
-        send,
-        s1,
+    g1, total1 = lax.optimization_barrier((g1, total1))
+    g2 = partner(gram + g1, 2)
+    sources = (send, s1, s2, s3)
+    out, last = call(
+        near_out_kernel,
+        (shape((2 * UNIT, NV), bf16), shape((LINE * NB, UNIT), f32)),
+        *sources,
         t1,
         t23,
-        scratch=[pltpu.VMEM(half.shape, f32)],
-    )
-    g1, total1 = lax.optimization_barrier((g1, total1))
-    g2 = partner(gram + g1, 2)
-    out, bias23 = call(
-        near_out_kernel, (shape((2 * UNIT, NV), bf16), half), s2, s3, t1, t23, total1, total3
+        total1,
+        bias,
     )
     r1 = exchange(out, 1, 0)
-    own, mine = call(near_in_kernel, (unit, unit), send, s2, s3, t23, own, total2, bias23)
+    own, mine = call(near_in_kernel, (unit, unit), *sources, t23, own, bias, last)
     relayed = call(relay_kernel, shape((UNIT, NV), bf16), mine, r1)
     r2 = exchange(relayed, 3, 0)
     gram, own = lax.optimization_barrier((gram, own))

time: 52.9 us -> 53 us (level)
  the two profiles are of different devices: /device:TPU:8 before, /device:TPU:2 now
where the time goes in v4:
time: 53 us; the launch traced here: 52.6 us
  starting transfers between devices  23.4 us (44%)
  waiting for transfers between devices  16 us (30%)
  Pallas kernels  12.3 us (23%)
  between operations  0.82 us (2%)
    ppermute x7, starting transfers between devices, exchange(): return lax.ppermute(value, ('row', 'col'), pairs)  19.6 us
    ppermute x7, waiting for transfers between devices, exchange(): return lax.ppermute(value, ('row', 'col'), pairs)  14.8 us
    pallas_call x8, Pallas kernels, call(): pl.pallas_call(kernel, out_shape=shapes, in_specs=[pl.BlockSpec(memory_sp...  12.3 us
    ppermute x2, starting transfers between devices, partner(): lax.ppermute(value, 'col', [(c, c ^ mask) for c in range(lax.axis_size('c...  3.84 us
    ppermute x2, waiting for transfers between devices, partner(): lax.ppermute(value, 'col', [(c, c ^ mask) for c in range(lax.axis_size('c...  1.18 us
  transfers between devices with their start and end apart: 9, of which 5 were waited for; matrix products, arithmetic and copies ran while one was open for 0% of the time, Pallas kernels for 19%

profile of v4, /device:TPU:2, one launch (start us, length us, event | category | flops | bytes accessed | tf_op | source)
XLA Modules:
  0.0 52.6 jit_solution(15856269863229955883)
XLA Ops:
  0.6 0.0 copy-start
  0.6 7.9 %collective-permute-start = (bf16[512,256]{1,0:T(8,128)(2,1)}, bf16[512,256]{1,0:T(8,128)(2,1)S(1)}, u32[]{:S(2)}, u32[]{:S(2)}) collective-permute-start(bf16[512,256]{1,0:T(8,128)(2,1)} %points.3), channel_id=1, source_target_pairs={{0,32},{1,129},{2,34},{3,131},{4,36},{5,133},{6,38},{7,135},{8,40}... | collective-permute-start | bytes 786440 | tf_op jit(solution)/shard_map/ppermute | solution.py:241
  8.6 1.9 %shard_map.60.s0 = bf16[528,384]{1,0:T(8,128)(2,1)} custom-call(bf16[512,256]{1,0:T(8,128)(2,1)} %points.3, bf16[512,128]{1,0:T(8,128)(2,1)} %weights.1, s32[4,16]{1,0:T(4,128)} %near.1), custom_call_target="tpu_custom_call" | custom-call | flops 1000000000 | bytes 3000000 | tf_op jit(solution)/shard_map/pallas_call | solution.py:221
  10.5 0.0 copy-start.2
  10.5 1.9 %collective-permute-start.1 = (bf16[528,384]{1,0:T(8,128)(2,1)}, bf16[528,384]{1,0:T(8,128)(2,1)S(1)}, u32[]{:S(2)}, u32[]{:S(2)}) collective-permute-start(bf16[528,384]{1,0:T(8,128)(2,1)} %shard_map.60.s0), channel_id=1, source_target_pairs={{0,384},{1,97},{2,386},{3,99},{4,388},{5,101},{6,390},{7,103},{8,3... | collective-permute-start | bytes 1216520 | tf_op jit(solution)/shard_map/ppermute | solution.py:241
  12.5 1.9 %collective-permute-start.2 = (bf16[528,384]{1,0:T(8,128)(2,1)}, bf16[528,384]{1,0:T(8,128)(2,1)S(1)}, u32[]{:S(2)}, u32[]{:S(2)}) collective-permute-start(bf16[528,384]{1,0:T(8,128)(2,1)} %shard_map.60.s0), channel_id=1, source_target_pairs={{0,128},{1,33},{2,130},{3,35},{4,132},{5,37},{6,134},{7,39},{8,136... | collective-permute-start | bytes 1216520 | tf_op jit(solution)/shard_map/ppermute | solution.py:241
  14.4 0.0 collective-permute-done.t1
  14.4 0.0 copy-done
  14.5 0.0 copy-start.1
  14.5 2.1 %collective-permute-start.4 = (bf16[1024,256]{1,0:T(8,128)(2,1)S(1)}, bf16[1024,256]{1,0:T(8,128)(2,1)S(1)}, u32[]{:S(2)}, u32[]{:S(2)}) collective-permute-start(bf16[1024,256]{1,0:T(8,128)(2,1)S(1)} %pad_maximum_fusion), channel_id=1, source_target_pairs={{0,96},{1,385},{2,98},{3,387},{4,100},{5,389},{6,102},{7,391},{8,1... | collective-permute-start | bytes 1572872 | tf_op jit(solution)/shard_map/ppermute | solution.py:241
  16.5 0.0 copy-done.2
  16.5 0.8 %shard_map.59 = (f32[64,64]{1,0:T(8,128)S(1)}, f32[512,128]{1,0:T(8,128)S(1)}) custom-call(bf16[512,256]{1,0:T(8,128)(2,1)S(1)} %copy-done, bf16[64,256]{1,0:T(8,128)(2,1)S(1)} %copy-done.2), custom_call_target="tpu_custom_call" | custom-call | flops 1000000000 | bytes 3000000 | tf_op jit(solution)/shard_map/pallas_call | solution.py:221
  17.3 8.0 %collective-permute-done.1.s1 = bf16[528,384]{1,0:T(8,128)(2,1)S(1)} collective-permute-done((bf16[528,384]{1,0:T(8,128)(2,1)}, bf16[528,384]{1,0:T(8,128)(2,1)S(1)}, u32[]{:S(2)}, u32[]{:S(2)}) %collective-permute-start.1) | collective-permute-done | bytes 405536 | tf_op jit(solution)/shard_map/ppermute | solution.py:241
  25.3 1.9 %collective-permute-start.3 = (bf16[528,384]{1,0:T(8,128)(2,1)S(1)}, bf16[528,384]{1,0:T(8,128)(2,1)S(1)}, u32[]{:S(2)}, u32[]{:S(2)}) collective-permute-start(bf16[528,384]{1,0:T(8,128)(2,1)S(1)} %collective-permute-done.1.s1), channel_id=1, source_target_pairs={{0,128},{1,33},{2,130},{3,35},{4,132},{5,37},{6,134},{7,39},{8,136... | collective-permute-start | bytes 1216520 | tf_op jit(solution)/shard_map/ppermute | solution.py:241
  27.2 0.0 collective-permute-done.2.s2
  27.2 0.0 copy-done.1
  27.3 2.2 %shard_map.61 = (f32[512,128]{1,0:T(8,128)S(1)}, f32[512,128]{1,0:T(8,128)S(1)}, f32[16,1536]{1,0:T(8,128)S(1)}) custom-call(bf16[528,384]{1,0:T(8,128)(2,1)S(1)} %copy-done.1, bf16[528,384]{1,0:T(8,128)(2,1)S(1)} %collective-permute-done.1.s1, bf16[528,384]{1,0:T(8,128)(2,1)S(1)} %collective-permute-done.2.s2, bf16[512,256]{1,0:T(8,128)(2,1)S(1)} %collective-permute-done.t1), custom_call_target="tpu_custom_call" | custom-call | flops 20000000000 | bytes 60000000 | tf_op jit(solution)/shard_map/pallas_call | solution.py:221
  29.5 1.9 %collective-permute-start.5 = (f32[64,64]{1,0:T(8,128)S(1)}, f32[64,64]{1,0:T(8,128)S(1)}, u32[]{:S(2)}, u32[]{:S(2)}) collective-permute-start(f32[64,64]{1,0:T(8,128)S(1)} %get-tuple-element.34.g0), channel_id=1, source_target_pairs={{0,1},{1,0},{2,3},{3,2},{4,5},{5,4},{6,7},{7,6},{8,9},{9,8},{10,11... | collective-permute-start | bytes 49160 | tf_op jit(solution)/shard_map/ppermute | solution.py:245
  31.4 1.2 %collective-permute-done.5.s1 = f32[64,64]{1,0:T(8,128)S(1)} collective-permute-done((f32[64,64]{1,0:T(8,128)S(1)}, f32[64,64]{1,0:T(8,128)S(1)}, u32[]{:S(2)}, u32[]{:S(2)}) %collective-permute-start.5) | collective-permute-done | bytes 16416 | tf_op jit(solution)/shard_map/ppermute | solution.py:245
  32.6 0.0 collective-permute-done.4.t23
  32.6 2.5 %collective-permute-done.3.s3 = bf16[528,384]{1,0:T(8,128)(2,1)S(1)} collective-permute-done((bf16[528,384]{1,0:T(8,128)(2,1)S(1)}, bf16[528,384]{1,0:T(8,128)(2,1)S(1)}, u32[]{:S(2)}, u32[]{:S(2)}) %collective-permute-start.3) | collective-permute-done | bytes 405536 | tf_op jit(solution)/shard_map/ppermute | solution.py:241
  35.1 1.6 %shard_map.62 = (bf16[1024,128]{1,0:T(8,128)(2,1)S(1)}, f32[16,512]{1,0:T(8,128)S(1)}) custom-call(bf16[528,384]{1,0:T(8,128)(2,1)S(1)} %copy-done.1, bf16[528,384]{1,0:T(8,128)(2,1)S(1)} %collective-permute-done.1.s1, bf16[528,384]{1,0:T(8,128)(2,1)S(1)} %collective-permute-done.2.s2, bf16[528,384]{1,0:T(8,128)(2,1)S(1)} %collective-permute-done.3.s3, ...), custom_call_target="tpu_custom_call" | custom-call | flops 1000000000 | bytes 3000000 | tf_op jit(solution)/shard_map/pallas_call | solution.py:221
  36.7 1.9 %collective-permute-start.6 = (bf16[1024,128]{1,0:T(8,128)(2,1)S(1)}, bf16[1024,128]{1,0:T(8,128)(2,1)S(1)}, u32[]{:S(2)}, u32[]{:S(2)}) collective-permute-start(bf16[1024,128]{1,0:T(8,128)(2,1)S(1)} %get-tuple-element.31), channel_id=1, source_target_pairs={{0,32},{1,129},{2,34},{3,131},{4,36},{5,133},{6,38},{7,135},{8,40}... | collective-permute-start | bytes 786440 | tf_op jit(solution)/shard_map/ppermute | solution.py:241
  38.6 1.9 %collective-permute-start.8 = (f32[64,64]{1,0:T(8,128)S(1)}, f32[64,64]{1,0:T(8,128)S(1)}, u32[]{:S(2)}, u32[]{:S(2)}) collective-permute-start(f32[64,64]{1,0:T(8,128)S(1)} %add.3), channel_id=1, source_target_pairs={{0,2},{1,3},{2,0},{3,1},{4,6},{5,7},{6,4},{7,5},{8,10},{9,11},{10,... | collective-permute-start | bytes 49160 | tf_op jit(solution)/shard_map/ppermute | solution.py:245
  40.6 1.6 %shard_map.63 = (f32[512,128]{1,0:T(8,128)S(1)}, f32[512,128]{1,0:T(8,128)S(1)}) custom-call(bf16[528,384]{1,0:T(8,128)(2,1)S(1)} %copy-done.1, bf16[528,384]{1,0:T(8,128)(2,1)S(1)} %collective-permute-done.1.s1, bf16[528,384]{1,0:T(8,128)(2,1)S(1)} %collective-permute-done.2.s2, bf16[528,384]{1,0:T(8,128)(2,1)S(1)} %collective-permute-done.3.s3, ...), custom_call_target="tpu_custom_call" | custom-call | flops 1000000000 | bytes 3000000 | tf_op jit(solution)/shard_map/pallas_call | solution.py:221
  42.1 2.8 %collective-permute-done.6.received.first = bf16[1024,128]{1,0:T(8,128)(2,1)S(1)} collective-permute-done((bf16[1024,128]{1,0:T(8,128)(2,1)S(1)}, bf16[1024,128]{1,0:T(8,128)(2,1)S(1)}, u32[]{:S(2)}, u32[]{:S(2)}) %collective-permute-start.6) | collective-permute-done | bytes 262176 | tf_op jit(solution)/shard_map/ppermute | solution.py:241
  45.0 1.9 %collective-permute-start.7 = (bf16[512,128]{1,0:T(8,128)(2,1)S(1)}, bf16[512,128]{1,0:T(8,128)(2,1)S(1)}, u32[]{:S(2)}, u32[]{:S(2)}) collective-permute-start(bf16[512,128]{1,0:T(8,128)(2,1)S(1)} %shard_map.64), channel_id=1, source_target_pairs={{0,96},{1,385},{2,98},{3,387},{4,100},{5,389},{6,102},{7,391},{8,1... | collective-permute-start | bytes 393224 | tf_op jit(solution)/shard_map/ppermute | solution.py:241
  46.9 0.0 collective-permute-done.8.s2
  46.9 3.4 %shard_map.66 = f32[64,192]{1,0:T(8,128)} custom-call(f32[64,64]{1,0:T(8,128)S(1)} %get-tuple-element.34.g0, f32[64,64]{1,0:T(8,128)S(1)} %collective-permute-done.5.s1, f32[64,64]{1,0:T(8,128)S(1)} %collective-permute-done.8.s2), custom_call_target="tpu_custom_call" | custom-call | flops 3400000000 | bytes 10200000 | tf_op jit(solution)/shard_map/pallas_call | solution.py:221
  50.4 1.5 %collective-permute-done.7.second = bf16[512,128]{1,0:T(8,128)(2,1)S(1)} collective-permute-done((bf16[512,128]{1,0:T(8,128)(2,1)S(1)}, bf16[512,128]{1,0:T(8,128)(2,1)S(1)}, u32[]{:S(2)}, u32[]{:S(2)}) %collective-permute-start.7) | collective-permute-done | bytes 131104 | tf_op jit(solution)/shard_map/ppermute | solution.py:241
  51.8 0.7 %shard_map.65 = bf16[512,128]{1,0:T(8,128)(2,1)} custom-call(f32[512,128]{1,0:T(8,128)S(1)} %get-tuple-element.30.own, bf16[1024,128]{1,0:T(8,128)(2,1)S(1)} %collective-permute-done.6.received.first, bf16[512,128]{1,0:T(8,128)(2,1)S(1)} %collective-permute-done.7.second, f32[512,128]{1,0:T(8,128)S(1)} %get-tuple-element.33.scale), custom_call_target="tpu_custom_call" | custom-call | flops 1000000000 | bytes 3000000 | tf_op jit(solution)/shard_map/pallas_call | solution.py:221
  (3 shorter events, 0.1 us)
Async XLA Ops:
  0.6 13.8 %copy-start = (bf16[512,256]{1,0:T(8,128)(2,1)S(1)}, bf16[512,256]{1,0:T(8,128)(2,1)}, u32[]{:S(2)}) copy-start(bf16[512,256]{1,0:T(8,128)(2,1)} %points.3) | copy-start | bytes 786436
  0.6 13.8 %collective-permute-start = (bf16[512,256]{1,0:T(8,128)(2,1)}, bf16[512,256]{1,0:T(8,128)(2,1)S(1)}, u32[]{:S(2)}, u32[]{:S(2)}) collective-permute-start(bf16[512,256]{1,0:T(8,128)(2,1)} %points.3), channel_id=1, source_target_pairs={{0,32},{1,129},{2,34},{3,131},{4,36},{5,133},{6,38},{7,135},{8,40}... | collective-permute-start | bytes 786440 | tf_op jit(solution)/shard_map/ppermute | solution.py:241
  10.5 6.0 %copy-start.2 = (bf16[64,256]{1,0:T(8,128)(2,1)S(1)}, bf16[64,256]{1,0:T(8,128)(2,1)}, u32[]{:S(2)}) copy-start(bf16[64,256]{1,0:T(8,128)(2,1)} %proxies) | copy-start | bytes 98308
  10.5 14.8 %collective-permute-start.1 = (bf16[528,384]{1,0:T(8,128)(2,1)}, bf16[528,384]{1,0:T(8,128)(2,1)S(1)}, u32[]{:S(2)}, u32[]{:S(2)}) collective-permute-start(bf16[528,384]{1,0:T(8,128)(2,1)} %shard_map.60.s0), channel_id=1, source_target_pairs={{0,384},{1,97},{2,386},{3,99},{4,388},{5,101},{6,390},{7,103},{8,3... | collective-permute-start | bytes 1216520 | tf_op jit(solution)/shard_map/ppermute | solution.py:241
  12.5 14.8 %collective-permute-start.2 = (bf16[528,384]{1,0:T(8,128)(2,1)}, bf16[528,384]{1,0:T(8,128)(2,1)S(1)}, u32[]{:S(2)}, u32[]{:S(2)}) collective-permute-start(bf16[528,384]{1,0:T(8,128)(2,1)} %shard_map.60.s0), channel_id=1, source_target_pairs={{0,128},{1,33},{2,130},{3,35},{4,132},{5,37},{6,134},{7,39},{8,136... | collective-permute-start | bytes 1216520 | tf_op jit(solution)/shard_map/ppermute | solution.py:241
  14.5 12.8 %copy-start.1 = (bf16[528,384]{1,0:T(8,128)(2,1)S(1)}, bf16[528,384]{1,0:T(8,128)(2,1)}, u32[]{:S(2)}) copy-start(bf16[528,384]{1,0:T(8,128)(2,1)} %shard_map.60.s0) | copy-start | bytes 1216516
  14.5 18.1 %collective-permute-start.4 = (bf16[1024,256]{1,0:T(8,128)(2,1)S(1)}, bf16[1024,256]{1,0:T(8,128)(2,1)S(1)}, u32[]{:S(2)}, u32[]{:S(2)}) collective-permute-start(bf16[1024,256]{1,0:T(8,128)(2,1)S(1)} %pad_maximum_fusion), channel_id=1, source_target_pairs={{0,96},{1,385},{2,98},{3,387},{4,100},{5,389},{6,102},{7,391},{8,1... | collective-permute-start | bytes 1572872 | tf_op jit(solution)/shard_map/ppermute | solution.py:241
  25.3 9.8 %collective-permute-start.3 = (bf16[528,384]{1,0:T(8,128)(2,1)S(1)}, bf16[528,384]{1,0:T(8,128)(2,1)S(1)}, u32[]{:S(2)}, u32[]{:S(2)}) collective-permute-start(bf16[528,384]{1,0:T(8,128)(2,1)S(1)} %collective-permute-done.1.s1), channel_id=1, source_target_pairs={{0,128},{1,33},{2,130},{3,35},{4,132},{5,37},{6,134},{7,39},{8,136... | collective-permute-start | bytes 1216520 | tf_op jit(solution)/shard_map/ppermute | solution.py:241
  29.5 3.1 %collective-permute-start.5 = (f32[64,64]{1,0:T(8,128)S(1)}, f32[64,64]{1,0:T(8,128)S(1)}, u32[]{:S(2)}, u32[]{:S(2)}) collective-permute-start(f32[64,64]{1,0:T(8,128)S(1)} %get-tuple-element.34.g0), channel_id=1, source_target_pairs={{0,1},{1,0},{2,3},{3,2},{4,5},{5,4},{6,7},{7,6},{8,9},{9,8},{10,11... | collective-permute-start | bytes 49160 | tf_op jit(solution)/shard_map/ppermute | solution.py:245
  36.7 8.3 %collective-permute-start.6 = (bf16[1024,128]{1,0:T(8,128)(2,1)S(1)}, bf16[1024,128]{1,0:T(8,128)(2,1)S(1)}, u32[]{:S(2)}, u32[]{:S(2)}) collective-permute-start(bf16[1024,128]{1,0:T(8,128)(2,1)S(1)} %get-tuple-element.31), channel_id=1, source_target_pairs={{0,32},{1,129},{2,34},{3,131},{4,36},{5,133},{6,38},{7,135},{8,40}... | collective-permute-start | bytes 786440 | tf_op jit(solution)/shard_map/ppermute | solution.py:241
  38.6 8.3 %collective-permute-start.8 = (f32[64,64]{1,0:T(8,128)S(1)}, f32[64,64]{1,0:T(8,128)S(1)}, u32[]{:S(2)}, u32[]{:S(2)}) collective-permute-start(f32[64,64]{1,0:T(8,128)S(1)} %add.3), channel_id=1, source_target_pairs={{0,2},{1,3},{2,0},{3,1},{4,6},{5,7},{6,4},{7,5},{8,10},{9,11},{10,... | collective-permute-start | bytes 49160 | tf_op jit(solution)/shard_map/ppermute | solution.py:245
  45.0 6.9 %collective-permute-start.7 = (bf16[512,128]{1,0:T(8,128)(2,1)S(1)}, bf16[512,128]{1,0:T(8,128)(2,1)S(1)}, u32[]{:S(2)}, u32[]{:S(2)}) collective-permute-start(bf16[512,128]{1,0:T(8,128)(2,1)S(1)} %shard_map.64), channel_id=1, source_target_pairs={{0,96},{1,385},{2,98},{3,387},{4,100},{5,389},{6,102},{7,391},{8,1... | collective-permute-start | bytes 393224 | tf_op jit(solution)/shard_map/ppermute | solution.py:241

commit v5 on v3

--- a/solution.py
+++ b/solution.py
@@ -20,7 +20,7 @@
 GROUP = 64
 LOG2E = 1.4426950408889634
 LINE = 4
-MASKS = (0, 1, 3, 2)
+MASKS = (0, 3, 1, 2)
 PANEL = 4
 NT = (((1,), (1,)), ((), ()))
 HIGH = lax.Precision.HIGHEST
@@ -248,7 +248,7 @@
 def on_device(points, weights, near_blocks, proxies):
     f32, bf16 = jnp.float32, jnp.bfloat16
     shape = jax.ShapeDtypeStruct
-    t1 = exchange(points, 1, 0)
+    t1 = exchange(points, 3, 0)
     send = call(
         send_kernel,
         shape((ROWS, DIM + NV), bf16),
@@ -265,7 +265,7 @@
     )
     s1 = exchange(send, 3, 1)
     s2 = exchange(send, 1, 1)
-    t23 = exchange(jnp.concatenate([points, t1], axis=0), 3, 0)
+    t23 = exchange(jnp.concatenate([points, t1], axis=0), 1, 0)
     proxies, t1 = lax.optimization_barrier((proxies, t1))
     gram, scale = call(gram_kernel, (shape((RANK, RANK), f32), shape((UNIT, NV), f32)), points, proxies)
     s3 = exchange(s1, 1, 1)
@@ -287,10 +287,10 @@
     out, bias23 = call(
         near_out_kernel, (shape((2 * UNIT, NV), bf16), half), s2, s3, t1, t23, total1, total3
     )
-    r1 = exchange(out, 1, 0)
+    r1 = exchange(out, 3, 0)
     own, mine = call(near_in_kernel, (unit, unit), send, s2, s3, t23, own, total2, bias23)
     relayed = call(relay_kernel, shape((UNIT, NV), bf16), mine, r1)
-    r2 = exchange(relayed, 3, 0)
+    r2 = exchange(relayed, 1, 0)
     gram, own = lax.optimization_barrier((gram, own))
     factors = call(factor_kernel, shape((RANK, 3 * RANK), f32), gram, g1, g2, micros=3.4)
     near_product = call(finish_kernel, shape((UNIT, NV), bf16), own, r1, r2, scale)

time: 52.9 us -> 54.7 us (1.034)
  the two profiles are of different devices: /device:TPU:8 before, /device:TPU:2 now
where the time goes in v5:
time: 54.7 us; the launch traced here: 54.3 us
  starting transfers between devices  35 us (64%)
  Pallas kernels  12.6 us (23%)
  waiting for transfers between devices  5.88 us (11%)
  between operations  0.84 us (2%)
    ppermute x7, starting transfers between devices, exchange(): return lax.ppermute(value, ('row', 'col'), pairs)  31.1 us
    pallas_call x8, Pallas kernels, call(): pl.pallas_call(kernel, out_shape=shapes, in_specs=[pl.BlockSpec(memory_sp...  12.6 us
    ppermute x7, waiting for transfers between devices, exchange(): return lax.ppermute(value, ('row', 'col'), pairs)  5.87 us
    ppermute x2, starting transfers between devices, partner(): lax.ppermute(value, 'col', [(c, c ^ mask) for c in range(lax.axis_size('c...  3.85 us
  transfers between devices with their start and end apart: 9, of which 2 were waited for; matrix products, arithmetic and copies ran while one was open for 0% of the time, Pallas kernels for 19%

profile of v5, /device:TPU:2, one launch (start us, length us, event | category | flops | bytes accessed | tf_op | source)
XLA Modules:
  0.0 54.3 jit_solution(8103597720905029452)
XLA Ops:
  0.6 0.0 copy-start
  0.6 3.5 %collective-permute-start = (bf16[512,256]{1,0:T(8,128)(2,1)}, bf16[512,256]{1,0:T(8,128)(2,1)S(1)}, u32[]{:S(2)}, u32[]{:S(2)}) collective-permute-start(bf16[512,256]{1,0:T(8,128)(2,1)} %points.3), channel_id=1, source_target_pairs={{0,96},{1,385},{2,98},{3,387},{4,100},{5,389},{6,102},{7,391},{8,1... | collective-permute-start | bytes 786440 | tf_op jit(solution)/shard_map/ppermute | solution.py:241
  4.2 1.9 %shard_map.60.s0 = bf16[528,384]{1,0:T(8,128)(2,1)} custom-call(bf16[512,256]{1,0:T(8,128)(2,1)} %points.3, bf16[512,128]{1,0:T(8,128)(2,1)} %weights.1, s32[4,16]{1,0:T(4,128)} %near.1), custom_call_target="tpu_custom_call" | custom-call | flops 1000000000 | bytes 3000000 | tf_op jit(solution)/shard_map/pallas_call | solution.py:221
  6.1 0.0 copy-start.1
  6.1 0.0 copy-start.2
  6.1 5.1 %collective-permute-start.1 = (bf16[528,384]{1,0:T(8,128)(2,1)}, bf16[528,384]{1,0:T(8,128)(2,1)S(1)}, u32[]{:S(2)}, u32[]{:S(2)}) collective-permute-start(bf16[528,384]{1,0:T(8,128)(2,1)} %shard_map.60.s0), channel_id=1, source_target_pairs={{0,384},{1,97},{2,386},{3,99},{4,388},{5,101},{6,390},{7,103},{8,3... | collective-permute-start | bytes 1216520 | tf_op jit(solution)/shard_map/ppermute | solution.py:241
  11.2 0.0 collective-permute-done.t1
  11.2 0.0 copy-done
  11.3 9.6 %collective-permute-start.4 = (bf16[1024,256]{1,0:T(8,128)(2,1)S(1)}, bf16[1024,256]{1,0:T(8,128)(2,1)S(1)}, u32[]{:S(2)}, u32[]{:S(2)}) collective-permute-start(bf16[1024,256]{1,0:T(8,128)(2,1)S(1)} %pad_maximum_fusion), channel_id=1, source_target_pairs={{0,32},{1,129},{2,34},{3,131},{4,36},{5,133},{6,38},{7,135},{8,40}... | collective-permute-start | bytes 1572872 | tf_op jit(solution)/shard_map/ppermute | solution.py:241
  20.9 0.0 copy-done.1
  20.9 1.9 %collective-permute-start.2 = (bf16[528,384]{1,0:T(8,128)(2,1)S(1)}, bf16[528,384]{1,0:T(8,128)(2,1)S(1)}, u32[]{:S(2)}, u32[]{:S(2)}) collective-permute-start(bf16[528,384]{1,0:T(8,128)(2,1)S(1)} %copy-done.1), channel_id=1, source_target_pairs={{0,128},{1,33},{2,130},{3,35},{4,132},{5,37},{6,134},{7,39},{8,136... | collective-permute-start | bytes 1216520 | tf_op jit(solution)/shard_map/ppermute | solution.py:241
  22.8 0.0 collective-permute-done.1.s1
  22.8 3.9 %collective-permute-start.3 = (bf16[528,384]{1,0:T(8,128)(2,1)S(1)}, bf16[528,384]{1,0:T(8,128)(2,1)S(1)}, u32[]{:S(2)}, u32[]{:S(2)}) collective-permute-start(bf16[528,384]{1,0:T(8,128)(2,1)S(1)} %collective-permute-done.1.s1), channel_id=1, source_target_pairs={{0,128},{1,33},{2,130},{3,35},{4,132},{5,37},{6,134},{7,39},{8,136... | collective-permute-start | bytes 1216520 | tf_op jit(solution)/shard_map/ppermute | solution.py:241
  26.8 0.0 copy-done.2
  26.8 0.8 %shard_map.59 = (f32[64,64]{1,0:T(8,128)S(1)}, f32[512,128]{1,0:T(8,128)S(1)}) custom-call(bf16[512,256]{1,0:T(8,128)(2,1)S(1)} %copy-done, bf16[64,256]{1,0:T(8,128)(2,1)S(1)} %copy-done.2), custom_call_target="tpu_custom_call" | custom-call | flops 1000000000 | bytes 3000000 | tf_op jit(solution)/shard_map/pallas_call | solution.py:221
  27.6 1.9 %collective-permute-start.5 = (f32[64,64]{1,0:T(8,128)S(1)}, f32[64,64]{1,0:T(8,128)S(1)}, u32[]{:S(2)}, u32[]{:S(2)}) collective-permute-start(f32[64,64]{1,0:T(8,128)S(1)} %get-tuple-element.36.g0), channel_id=1, source_target_pairs={{0,1},{1,0},{2,3},{3,2},{4,5},{5,4},{6,7},{7,6},{8,9},{9,8},{10,11... | collective-permute-start | bytes 49160 | tf_op jit(solution)/shard_map/ppermute | solution.py:245
  29.5 2.9 %collective-permute-done.4.t23 = bf16[1024,256]{1,0:T(8,128)(2,1)S(1)} collective-permute-done((bf16[1024,256]{1,0:T(8,128)(2,1)S(1)}, bf16[1024,256]{1,0:T(8,128)(2,1)S(1)}, u32[]{:S(2)}, u32[]{:S(2)}) %collective-permute-start.4) | collective-permute-done | bytes 524320 | tf_op jit(solution)/shard_map/ppermute | solution.py:241
  32.4 2.8 %shard_map.61 = (f32[512,128]{1,0:T(8,128)S(1)}, f32[512,128]{1,0:T(8,128)S(1)}, f32[512,128]{1,0:T(8,128)S(1)}, f32[512,128]{1,0:T(8,128)S(1)}) custom-call(bf16[528,384]{1,0:T(8,128)(2,1)S(1)} %copy-done.1, bf16[528,384]{1,0:T(8,128)(2,1)S(1)} %collective-permute-done.1.s1, bf16[512,256]{1,0:T(8,128)(2,1)S(1)} %collective-permute-done.t1, ...), custom_call_target="tpu_custom_call" | custom-call | flops 1000000000 | bytes 3000000 | tf_op jit(solution)/shard_map/pallas_call | solution.py:221
  35.2 0.0 collective-permute-done.5.s1
  35.2 0.0 collective-permute-done.2.s2
  35.2 0.0 collective-permute-done.3.s3
  35.2 1.5 %shard_map.62 = (bf16[1024,128]{1,0:T(8,128)(2,1)S(1)}, f32[16,1024]{1,0:T(8,128)S(1)}) custom-call(bf16[528,384]{1,0:T(8,128)(2,1)S(1)} %collective-permute-done.2.s2, bf16[528,384]{1,0:T(8,128)(2,1)S(1)} %collective-permute-done.3.s3, bf16[512,256]{1,0:T(8,128)(2,1)S(1)} %collective-permute-done.t1, bf16[1024,256]{1,0:T(8,128)(2,1)S(1)} %collective-permute-done.4.t23, ...), custom_call_target="tpu_custom_call" | custom-call | flops 1000000000 | bytes 3000000 | tf_op jit(solution)/shard_map/pallas_call | solution.py:221
  36.7 1.9 %collective-permute-start.6 = (bf16[1024,128]{1,0:T(8,128)(2,1)S(1)}, bf16[1024,128]{1,0:T(8,128)(2,1)S(1)}, u32[]{:S(2)}, u32[]{:S(2)}) collective-permute-start(bf16[1024,128]{1,0:T(8,128)(2,1)S(1)} %get-tuple-element.33), channel_id=1, source_target_pairs={{0,96},{1,385},{2,98},{3,387},{4,100},{5,389},{6,102},{7,391},{8,1... | collective-permute-start | bytes 786440 | tf_op jit(solution)/shard_map/ppermute | solution.py:241
  38.6 1.9 %collective-permute-start.8 = (f32[64,64]{1,0:T(8,128)S(1)}, f32[64,64]{1,0:T(8,128)S(1)}, u32[]{:S(2)}, u32[]{:S(2)}) collective-permute-start(f32[64,64]{1,0:T(8,128)S(1)} %add.3), channel_id=1, source_target_pairs={{0,2},{1,3},{2,0},{3,1},{4,6},{5,7},{6,4},{7,5},{8,10},{9,11},{10,... | collective-permute-start | bytes 49160 | tf_op jit(solution)/shard_map/ppermute | solution.py:245
  40.5 1.4 %shard_map.63 = (f32[512,128]{1,0:T(8,128)S(1)}, f32[512,128]{1,0:T(8,128)S(1)}) custom-call(bf16[528,384]{1,0:T(8,128)(2,1)S(1)} %copy-done.1, bf16[528,384]{1,0:T(8,128)(2,1)S(1)} %collective-permute-done.2.s2, bf16[528,384]{1,0:T(8,128)(2,1)S(1)} %collective-permute-done.3.s3, bf16[1024,256]{1,0:T(8,128)(2,1)S(1)} %collective-permute-done.4.t23, ...), custom_call_target="tpu_custom_call" | custom-call | flops 1000000000 | bytes 3000000 | tf_op jit(solution)/shard_map/pallas_call | solution.py:221
  41.9 3.0 %collective-permute-done.6.received.first = bf16[1024,128]{1,0:T(8,128)(2,1)S(1)} collective-permute-done((bf16[1024,128]{1,0:T(8,128)(2,1)S(1)}, bf16[1024,128]{1,0:T(8,128)(2,1)S(1)}, u32[]{:S(2)}, u32[]{:S(2)}) %collective-permute-start.6) | collective-permute-done | bytes 262176 | tf_op jit(solution)/shard_map/ppermute | solution.py:241
  45.0 5.1 %collective-permute-start.7 = (bf16[512,128]{1,0:T(8,128)(2,1)S(1)}, bf16[512,128]{1,0:T(8,128)(2,1)S(1)}, u32[]{:S(2)}, u32[]{:S(2)}) collective-permute-start(bf16[512,128]{1,0:T(8,128)(2,1)S(1)} %shard_map.64), channel_id=1, source_target_pairs={{0,32},{1,129},{2,34},{3,131},{4,36},{5,133},{6,38},{7,135},{8,40}... | collective-permute-start | bytes 393224 | tf_op jit(solution)/shard_map/ppermute | solution.py:241
  50.1 0.0 collective-permute-done.8.s2
  50.1 3.4 %shard_map.66 = f32[64,192]{1,0:T(8,128)} custom-call(f32[64,64]{1,0:T(8,128)S(1)} %get-tuple-element.36.g0, f32[64,64]{1,0:T(8,128)S(1)} %collective-permute-done.5.s1, f32[64,64]{1,0:T(8,128)S(1)} %collective-permute-done.8.s2), custom_call_target="tpu_custom_call" | custom-call | flops 3400000000 | bytes 10200000 | tf_op jit(solution)/shard_map/pallas_call | solution.py:221
  53.6 0.0 collective-permute-done.7.second
  53.6 0.7 %shard_map.65 = bf16[512,128]{1,0:T(8,128)(2,1)} custom-call(f32[512,128]{1,0:T(8,128)S(1)} %get-tuple-element.32.own, bf16[1024,128]{1,0:T(8,128)(2,1)S(1)} %collective-permute-done.6.received.first, bf16[512,128]{1,0:T(8,128)(2,1)S(1)} %collective-permute-done.7.second, f32[512,128]{1,0:T(8,128)S(1)} %get-tuple-element.35.scale), custom_call_target="tpu_custom_call" | custom-call | flops 1000000000 | bytes 3000000 | tf_op jit(solution)/shard_map/pallas_call | solution.py:221
  (3 shorter events, 0.1 us)
Async XLA Ops:
  0.6 10.6 %copy-start = (bf16[512,256]{1,0:T(8,128)(2,1)S(1)}, bf16[512,256]{1,0:T(8,128)(2,1)}, u32[]{:S(2)}) copy-start(bf16[512,256]{1,0:T(8,128)(2,1)} %points.3) | copy-start | bytes 786436
  0.6 10.6 %collective-permute-start = (bf16[512,256]{1,0:T(8,128)(2,1)}, bf16[512,256]{1,0:T(8,128)(2,1)S(1)}, u32[]{:S(2)}, u32[]{:S(2)}) collective-permute-start(bf16[512,256]{1,0:T(8,128)(2,1)} %points.3), channel_id=1, source_target_pairs={{0,96},{1,385},{2,98},{3,387},{4,100},{5,389},{6,102},{7,391},{8,1... | collective-permute-start | bytes 786440 | tf_op jit(solution)/shard_map/ppermute | solution.py:241
  6.1 14.8 %copy-start.1 = (bf16[528,384]{1,0:T(8,128)(2,1)S(1)}, bf16[528,384]{1,0:T(8,128)(2,1)}, u32[]{:S(2)}) copy-start(bf16[528,384]{1,0:T(8,128)(2,1)} %shard_map.60.s0) | copy-start | bytes 1216516
  6.1 20.7 %copy-start.2 = (bf16[64,256]{1,0:T(8,128)(2,1)S(1)}, bf16[64,256]{1,0:T(8,128)(2,1)}, u32[]{:S(2)}) copy-start(bf16[64,256]{1,0:T(8,128)(2,1)} %proxies) | copy-start | bytes 98308
  6.1 16.7 %collective-permute-start.1 = (bf16[528,384]{1,0:T(8,128)(2,1)}, bf16[528,384]{1,0:T(8,128)(2,1)S(1)}, u32[]{:S(2)}, u32[]{:S(2)}) collective-permute-start(bf16[528,384]{1,0:T(8,128)(2,1)} %shard_map.60.s0), channel_id=1, source_target_pairs={{0,384},{1,97},{2,386},{3,99},{4,388},{5,101},{6,390},{7,103},{8,3... | collective-permute-start | bytes 1216520 | tf_op jit(solution)/shard_map/ppermute | solution.py:241
  11.3 21.1 %collective-permute-start.4 = (bf16[1024,256]{1,0:T(8,128)(2,1)S(1)}, bf16[1024,256]{1,0:T(8,128)(2,1)S(1)}, u32[]{:S(2)}, u32[]{:S(2)}) collective-permute-start(bf16[1024,256]{1,0:T(8,128)(2,1)S(1)} %pad_maximum_fusion), channel_id=1, source_target_pairs={{0,32},{1,129},{2,34},{3,131},{4,36},{5,133},{6,38},{7,135},{8,40}... | collective-permute-start | bytes 1572872 | tf_op jit(solution)/shard_map/ppermute | solution.py:241
  20.9 14.3 %collective-permute-start.2 = (bf16[528,384]{1,0:T(8,128)(2,1)S(1)}, bf16[528,384]{1,0:T(8,128)(2,1)S(1)}, u32[]{:S(2)}, u32[]{:S(2)}) collective-permute-start(bf16[528,384]{1,0:T(8,128)(2,1)S(1)} %copy-done.1), channel_id=1, source_target_pairs={{0,128},{1,33},{2,130},{3,35},{4,132},{5,37},{6,134},{7,39},{8,136... | collective-permute-start | bytes 1216520 | tf_op jit(solution)/shard_map/ppermute | solution.py:241
  22.8 12.4 %collective-permute-start.3 = (bf16[528,384]{1,0:T(8,128)(2,1)S(1)}, bf16[528,384]{1,0:T(8,128)(2,1)S(1)}, u32[]{:S(2)}, u32[]{:S(2)}) collective-permute-start(bf16[528,384]{1,0:T(8,128)(2,1)S(1)} %collective-permute-done.1.s1), channel_id=1, source_target_pairs={{0,128},{1,33},{2,130},{3,35},{4,132},{5,37},{6,134},{7,39},{8,136... | collective-permute-start | bytes 1216520 | tf_op jit(solution)/shard_map/ppermute | solution.py:241
  27.6 7.6 %collective-permute-start.5 = (f32[64,64]{1,0:T(8,128)S(1)}, f32[64,64]{1,0:T(8,128)S(1)}, u32[]{:S(2)}, u32[]{:S(2)}) collective-permute-start(f32[64,64]{1,0:T(8,128)S(1)} %get-tuple-element.36.g0), channel_id=1, source_target_pairs={{0,1},{1,0},{2,3},{3,2},{4,5},{5,4},{6,7},{7,6},{8,9},{9,8},{10,11... | collective-permute-start | bytes 49160 | tf_op jit(solution)/shard_map/ppermute | solution.py:245
  36.7 8.3 %collective-permute-start.6 = (bf16[1024,128]{1,0:T(8,128)(2,1)S(1)}, bf16[1024,128]{1,0:T(8,128)(2,1)S(1)}, u32[]{:S(2)}, u32[]{:S(2)}) collective-permute-start(bf16[1024,128]{1,0:T(8,128)(2,1)S(1)} %get-tuple-element.33), channel_id=1, source_target_pairs={{0,96},{1,385},{2,98},{3,387},{4,100},{5,389},{6,102},{7,391},{8,1... | collective-permute-start | bytes 786440 | tf_op jit(solution)/shard_map/ppermute | solution.py:241
  38.6 11.5 %collective-permute-start.8 = (f32[64,64]{1,0:T(8,128)S(1)}, f32[64,64]{1,0:T(8,128)S(1)}, u32[]{:S(2)}, u32[]{:S(2)}) collective-permute-start(f32[64,64]{1,0:T(8,128)S(1)} %add.3), channel_id=1, source_target_pairs={{0,2},{1,3},{2,0},{3,1},{4,6},{5,7},{6,4},{7,5},{8,10},{9,11},{10,... | collective-permute-start | bytes 49160 | tf_op jit(solution)/shard_map/ppermute | solution.py:245
  45.0 8.6 %collective-permute-start.7 = (bf16[512,128]{1,0:T(8,128)(2,1)S(1)}, bf16[512,128]{1,0:T(8,128)(2,1)S(1)}, u32[]{:S(2)}, u32[]{:S(2)}) collective-permute-start(bf16[512,128]{1,0:T(8,128)(2,1)S(1)} %shard_map.64), channel_id=1, source_target_pairs={{0,32},{1,129},{2,34},{3,131},{4,36},{5,133},{6,38},{7,135},{8,40}... | collective-permute-start | bytes 393224 | tf_op jit(solution)/shard_map/ppermute | solution.py:241
